TPU v7x, 32 devices: a whole 2x2x4 slice. The times are simulated.
32 devices in a mesh: wide: 16 (over z, y, core), narrow: 2 (over x).
Axes of the slice: x: 2, y: 2, z: 4, core: 2. Of those that a mesh axis runs over, the one named last changes fastest.
Arguments:
- fine_cot: float32 [2, 32, 128, 128], P(None, 'wide', 'narrow'), may hold values from -6 to 6
- obstacle: int32 [2, 32, 128, 128], P(None, 'wide', 'narrow'), may hold values 0 or 1
- sigma: float32 [32, 128, 128], P('wide', 'narrow'), may hold values from 0.2 to 20
Outputs:
- fine_adjoint: float32 [2, 32, 128, 128], P(None, 'wide', 'narrow')
- coarse_adjoint: float32 [16, 2, 16, 64], P('wide', 'narrow')
All inputs are finite; a program needn't handle non-finite values. No bound on the sum of `obstacle` on one device may be relied on, other than what follows from the above.
Results may differ from a plain program's by a relative error of at most 0.00011.
Values sent between devices are 32-bit elements; how exact they have to be, the bound alone decides.
A program may use at most 64 MiB of HBM per device.

v0:
```python
import jax
import jax.numpy as jnp
from jax import lax
from jax.sharding import PartitionSpec as P

SWEEPS = 4


OMEGA = 0.8
COEF_X = 1.0
COEF_Y = 1.0
COEF_Z = 4.0
SHIFT = 0.02


def with_halo(cells, sides, width):
    for axis, dim in sides:
        count = lax.axis_size(axis)
        ends = count - 1
        head = lax.slice_in_dim(cells, 0, width, axis=dim)
        tail = lax.slice_in_dim(cells, cells.shape[dim] - width, cells.shape[dim], axis=dim)
        cells = jnp.concatenate(
            [
                lax.ppermute(tail, axis, [(i, (i + 1) % count) for i in range(ends)]),
                cells,
                lax.ppermute(head, axis, [((i + 1) % count, i) for i in range(ends)]),
            ],
            axis=dim,
        )
    return cells


def sine_table(rows, cols, count):
    product = (rows[:, None] + 1) * (cols[None, :] + 1) % (2 * (count + 1))
    angle = jnp.pi * product.astype(jnp.float32) / (count + 1)
    return jnp.sqrt(2.0 / (count + 1)) * jnp.sin(angle)


def eigen_values(index, count):
    return 2.0 - 2.0 * jnp.cos(jnp.pi * (index + 1).astype(jnp.float32) / (count + 1))


def plane_transform(field):
    count_z = field.shape[2]
    count_y = field.shape[3]
    index_y = jnp.arange(count_y, dtype=jnp.int32)
    index_z = jnp.arange(count_z, dtype=jnp.int32)
    high = lax.Precision.HIGHEST
    field = jnp.einsum(
        "xdzy,yv->xdzv", field, sine_table(index_y, index_y, count_y), precision=high
    )
    return jnp.einsum("xdzv,zw->xdwv", field, sine_table(index_z, index_z, count_z), precision=high)


def plane_denominator(count_z, count_y):
    index_y = jnp.arange(count_y, dtype=jnp.int32)
    index_z = jnp.arange(count_z, dtype=jnp.int32)
    return (
        COEF_Y * eigen_values(index_y, count_y)[None, :]
        + COEF_Z * eigen_values(index_z, count_z)[:, None]
        + SHIFT
    )


def body(fine_cot, obstacle, sigma):
    diag = 6.0 + sigma
    fluid = obstacle.astype(jnp.float32)
    grad = fine_cot
    for sweep in range(SWEEPS):
        weighted = OMEGA * fluid * grad / diag
        padded = with_halo(weighted, (("wide", 1), ("narrow", 2)), 1)
        beside = padded[:, 2:, 1:-1] + padded[:, :-2, 1:-1]
        beside = beside + padded[:, 1:-1, 2:] + padded[:, 1:-1, :-2]
        vertical = jnp.pad(weighted, ((0, 0), (0, 0), (0, 0), (1, 1)))
        beside = beside + vertical[..., 2:] + vertical[..., :-2]
        grad = grad - diag * weighted + beside
    dirs, cells_x, cells_y, cells_z = grad.shape
    coarse = grad.reshape(dirs, cells_x // 2, 2, cells_y // 2, 2, cells_z // 8, 8).sum(
        axis=(2, 4, 6)
    )
    coarse = jnp.transpose(coarse, (1, 0, 3, 2))
    regrouped = lax.all_to_all(coarse, "narrow", split_axis=1, concat_axis=3, tiled=True)
    spectrum = plane_transform(regrouped)
    slabs = spectrum.shape[0]
    total_x = lax.axis_size("wide") * slabs
    own_rows = lax.axis_index("wide") * slabs + jnp.arange(slabs, dtype=jnp.int32)
    plane = plane_denominator(spectrum.shape[2], spectrum.shape[3])
    high = lax.Precision.HIGHEST

    def accumulate(piece):
        columns = jnp.arange(piece.shape[0], dtype=jnp.int32)
        table = sine_table(own_rows, columns, total_x)
        return jnp.einsum("kx,xdwv->kdwv", table, piece, precision=high)

    modes = accumulate(lax.all_gather(spectrum, "wide", axis=0, tiled=True))
    denom = COEF_X * eigen_values(own_rows, total_x)[:, None, None, None] + plane[None, None]
    back = plane_transform(modes / denom)
    coarse_adjoint = accumulate(lax.all_gather(back, "wide", axis=0, tiled=True))
    return (grad, coarse_adjoint)


def solution(mesh):
    placed = (
        P(None, "wide", "narrow", None),
        P(None, "wide", "narrow", None),
        P("wide", "narrow", None),
    )
    return jax.shard_map(
        body,
        mesh=mesh,
        in_specs=placed,
        out_specs=(P(None, "wide", "narrow", None), P("wide", "narrow", None, None)),
        check_vma=False,
    )
```

profile of v0, /device:TPU:0, one launch (start us, length us, event | category | flops | bytes accessed | tf_op | source)
XLA Modules:
  0.0 119.1 jit_solution(6856023964625204232)
XLA Ops:
  0.6 0.9 broadcast_add_fusion
  1.6 0.9 multiply_divide_fusion.3
  2.5 1.3 %collective-permute-start = (f32[2,1,64,128]{3,2,1,0:T(8,128)S(1)}, f32[2,1,64,128]{3,2,1,0:T(8,128)S(1)}, u32[]{:S(2)}, u32[]{:S(2)}) collective-permute-start(f32[2,1,64,128]{3,2,1,0:T(8,128)S(1)} %get-tuple-element.25), channel_id=1, source_target_pairs={{2,0},{4,2},{6,4},{8,6},{10,8},{12,10},{14,12},{16,14},{18,16},{20... | collective-permute-start | bytes 196616 | tf_op jit(solution)/shard_map/ppermute | solution.py:26
  3.8 3.2 %collective-permute-start.1 = (f32[2,1,64,128]{3,2,1,0:T(8,128)S(1)}, f32[2,1,64,128]{3,2,1,0:T(8,128)S(1)}, u32[]{:S(2)}, u32[]{:S(2)}) collective-permute-start(f32[2,1,64,128]{3,2,1,0:T(8,128)S(1)} %get-tuple-element.24), channel_id=1, source_target_pairs={{0,2},{2,4},{4,6},{6,8},{8,10},{10,12},{12,14},{14,16},{16,18},{18... | collective-permute-start | bytes 196616 | tf_op jit(solution)/shard_map/ppermute | solution.py:24
  7.0 0.9 collective-permute-done.1
  7.9 1.3 %collective-permute-start.2 = (f32[2,4,1,128]{3,2,1,0:T(1,128)S(1)}, f32[2,4,1,128]{3,2,1,0:T(1,128)S(1)}, u32[]{:S(2)}, u32[]{:S(2)}) collective-permute-start(f32[2,4,1,128]{3,2,1,0:T(1,128)S(1)} %get-tuple-element.16), channel_id=1, source_target_pairs={{1,0},{3,2},{5,4},{7,6},{9,8},{11,10},{13,12},{15,14},{17,16},{19,... | collective-permute-start | bytes 12296 | tf_op jit(solution)/shard_map/ppermute | solution.py:26
  9.2 4.8 %collective-permute-start.3 = (f32[2,4,1,128]{3,2,1,0:T(1,128)S(1)}, f32[2,4,1,128]{3,2,1,0:T(1,128)S(1)}, u32[]{:S(2)}, u32[]{:S(2)}) collective-permute-start(f32[2,4,1,128]{3,2,1,0:T(1,128)S(1)} %get-tuple-element.17), channel_id=1, source_target_pairs={{0,1},{2,3},{4,5},{6,7},{8,9},{10,11},{12,13},{14,15},{16,17},{18,... | collective-permute-start | bytes 12296 | tf_op jit(solution)/shard_map/ppermute | solution.py:24
  14.0 1.3 %collective-permute-done.3 = f32[2,4,1,128]{3,2,1,0:T(1,128)S(1)} collective-permute-done((f32[2,4,1,128]{3,2,1,0:T(1,128)S(1)}, f32[2,4,1,128]{3,2,1,0:T(1,128)S(1)}, u32[]{:S(2)}, u32[]{:S(2)}) %collective-permute-start.3) | collective-permute-done | bytes 4128 | tf_op jit(solution)/shard_map/ppermute | solution.py:24
  15.5 1.3 %collective-permute-start.4 = (f32[2,1,64,128]{3,2,1,0:T(8,128)S(1)}, f32[2,1,64,128]{3,2,1,0:T(8,128)S(1)}, u32[]{:S(2)}, u32[]{:S(2)}) collective-permute-start(f32[2,1,64,128]{3,2,1,0:T(8,128)S(1)} %get-tuple-element.23), channel_id=1, source_target_pairs={{2,0},{4,2},{6,4},{8,6},{10,8},{12,10},{14,12},{16,14},{18,16},{20... | collective-permute-start | bytes 196616 | tf_op jit(solution)/shard_map/ppermute | solution.py:26
  16.8 4.1 %collective-permute-start.5 = (f32[2,1,64,128]{3,2,1,0:T(8,128)S(1)}, f32[2,1,64,128]{3,2,1,0:T(8,128)S(1)}, u32[]{:S(2)}, u32[]{:S(2)}) collective-permute-start(f32[2,1,64,128]{3,2,1,0:T(8,128)S(1)} %get-tuple-element.22), channel_id=1, source_target_pairs={{0,2},{2,4},{4,6},{6,8},{8,10},{10,12},{12,14},{14,16},{16,18},{18... | collective-permute-start | bytes 196616 | tf_op jit(solution)/shard_map/ppermute | solution.py:24
  21.0 0.9 collective-permute-done.5
  21.8 1.3 %collective-permute-start.6 = (f32[2,4,1,128]{3,2,1,0:T(1,128)S(1)}, f32[2,4,1,128]{3,2,1,0:T(1,128)S(1)}, u32[]{:S(2)}, u32[]{:S(2)}) collective-permute-start(f32[2,4,1,128]{3,2,1,0:T(1,128)S(1)} %get-tuple-element.14), channel_id=1, source_target_pairs={{1,0},{3,2},{5,4},{7,6},{9,8},{11,10},{13,12},{15,14},{17,16},{19,... | collective-permute-start | bytes 12296 | tf_op jit(solution)/shard_map/ppermute | solution.py:26
  23.1 4.5 %collective-permute-start.7 = (f32[2,4,1,128]{3,2,1,0:T(1,128)S(1)}, f32[2,4,1,128]{3,2,1,0:T(1,128)S(1)}, u32[]{:S(2)}, u32[]{:S(2)}) collective-permute-start(f32[2,4,1,128]{3,2,1,0:T(1,128)S(1)} %get-tuple-element.15), channel_id=1, source_target_pairs={{0,1},{2,3},{4,5},{6,7},{8,9},{10,11},{12,13},{14,15},{16,17},{18,... | collective-permute-start | bytes 12296 | tf_op jit(solution)/shard_map/ppermute | solution.py:24
  27.7 1.3 %collective-permute-done.7 = f32[2,4,1,128]{3,2,1,0:T(1,128)S(1)} collective-permute-done((f32[2,4,1,128]{3,2,1,0:T(1,128)S(1)}, f32[2,4,1,128]{3,2,1,0:T(1,128)S(1)}, u32[]{:S(2)}, u32[]{:S(2)}) %collective-permute-start.7) | collective-permute-done | bytes 4128 | tf_op jit(solution)/shard_map/ppermute | solution.py:24
  29.2 1.3 %collective-permute-start.8 = (f32[2,1,64,128]{3,2,1,0:T(8,128)S(1)}, f32[2,1,64,128]{3,2,1,0:T(8,128)S(1)}, u32[]{:S(2)}, u32[]{:S(2)}) collective-permute-start(f32[2,1,64,128]{3,2,1,0:T(8,128)S(1)} %get-tuple-element.21), channel_id=1, source_target_pairs={{2,0},{4,2},{6,4},{8,6},{10,8},{12,10},{14,12},{16,14},{18,16},{20... | collective-permute-start | bytes 196616 | tf_op jit(solution)/shard_map/ppermute | solution.py:26
  30.5 5.8 %collective-permute-start.9 = (f32[2,1,64,128]{3,2,1,0:T(8,128)S(1)}, f32[2,1,64,128]{3,2,1,0:T(8,128)S(1)}, u32[]{:S(2)}, u32[]{:S(2)}) collective-permute-start(f32[2,1,64,128]{3,2,1,0:T(8,128)S(1)} %get-tuple-element.20), channel_id=1, source_target_pairs={{0,2},{2,4},{4,6},{6,8},{8,10},{10,12},{12,14},{14,16},{16,18},{18... | collective-permute-start | bytes 196616 | tf_op jit(solution)/shard_map/ppermute | solution.py:24
  36.3 0.9 collective-permute-done.9
  37.2 1.3 %collective-permute-start.10 = (f32[2,4,1,128]{3,2,1,0:T(1,128)S(1)}, f32[2,4,1,128]{3,2,1,0:T(1,128)S(1)}, u32[]{:S(2)}, u32[]{:S(2)}) collective-permute-start(f32[2,4,1,128]{3,2,1,0:T(1,128)S(1)} %get-tuple-element.12), channel_id=1, source_target_pairs={{1,0},{3,2},{5,4},{7,6},{9,8},{11,10},{13,12},{15,14},{17,16},{19,... | collective-permute-start | bytes 12296 | tf_op jit(solution)/shard_map/ppermute | solution.py:26
  38.5 4.5 %collective-permute-start.11 = (f32[2,4,1,128]{3,2,1,0:T(1,128)S(1)}, f32[2,4,1,128]{3,2,1,0:T(1,128)S(1)}, u32[]{:S(2)}, u32[]{:S(2)}) collective-permute-start(f32[2,4,1,128]{3,2,1,0:T(1,128)S(1)} %get-tuple-element.13), channel_id=1, source_target_pairs={{0,1},{2,3},{4,5},{6,7},{8,9},{10,11},{12,13},{14,15},{16,17},{18,... | collective-permute-start | bytes 12296 | tf_op jit(solution)/shard_map/ppermute | solution.py:24
  43.0 1.3 %collective-permute-done.11 = f32[2,4,1,128]{3,2,1,0:T(1,128)S(1)} collective-permute-done((f32[2,4,1,128]{3,2,1,0:T(1,128)S(1)}, f32[2,4,1,128]{3,2,1,0:T(1,128)S(1)}, u32[]{:S(2)}, u32[]{:S(2)}) %collective-permute-start.11) | collective-permute-done | bytes 4128 | tf_op jit(solution)/shard_map/ppermute | solution.py:24
  44.5 1.3 %collective-permute-start.12 = (f32[2,1,64,128]{3,2,1,0:T(8,128)S(1)}, f32[2,1,64,128]{3,2,1,0:T(8,128)S(1)}, u32[]{:S(2)}, u32[]{:S(2)}) collective-permute-start(f32[2,1,64,128]{3,2,1,0:T(8,128)S(1)} %get-tuple-element.19), channel_id=1, source_target_pairs={{2,0},{4,2},{6,4},{8,6},{10,8},{12,10},{14,12},{16,14},{18,16},{20... | collective-permute-start | bytes 196616 | tf_op jit(solution)/shard_map/ppermute | solution.py:26
  45.8 6.0 %collective-permute-start.13 = (f32[2,1,64,128]{3,2,1,0:T(8,128)S(1)}, f32[2,1,64,128]{3,2,1,0:T(8,128)S(1)}, u32[]{:S(2)}, u32[]{:S(2)}) collective-permute-start(f32[2,1,64,128]{3,2,1,0:T(8,128)S(1)} %get-tuple-element.18), channel_id=1, source_target_pairs={{0,2},{2,4},{4,6},{6,8},{8,10},{10,12},{12,14},{14,16},{16,18},{18... | collective-permute-start | bytes 196616 | tf_op jit(solution)/shard_map/ppermute | solution.py:24
  51.9 0.9 collective-permute-done.13
  52.7 1.3 %collective-permute-start.14 = (f32[2,4,1,128]{3,2,1,0:T(1,128)S(1)}, f32[2,4,1,128]{3,2,1,0:T(1,128)S(1)}, u32[]{:S(2)}, u32[]{:S(2)}) collective-permute-start(f32[2,4,1,128]{3,2,1,0:T(1,128)S(1)} %get-tuple-element.10), channel_id=1, source_target_pairs={{1,0},{3,2},{5,4},{7,6},{9,8},{11,10},{13,12},{15,14},{17,16},{19,... | collective-permute-start | bytes 12296 | tf_op jit(solution)/shard_map/ppermute | solution.py:26
  54.0 4.5 %collective-permute-start.15 = (f32[2,4,1,128]{3,2,1,0:T(1,128)S(1)}, f32[2,4,1,128]{3,2,1,0:T(1,128)S(1)}, u32[]{:S(2)}, u32[]{:S(2)}) collective-permute-start(f32[2,4,1,128]{3,2,1,0:T(1,128)S(1)} %get-tuple-element.11), channel_id=1, source_target_pairs={{0,1},{2,3},{4,5},{6,7},{8,9},{10,11},{12,13},{14,15},{16,17},{18,... | collective-permute-start | bytes 12296 | tf_op jit(solution)/shard_map/ppermute | solution.py:24
  58.6 1.3 %collective-permute-done.15 = f32[2,4,1,128]{3,2,1,0:T(1,128)S(1)} collective-permute-done((f32[2,4,1,128]{3,2,1,0:T(1,128)S(1)}, f32[2,4,1,128]{3,2,1,0:T(1,128)S(1)}, u32[]{:S(2)}, u32[]{:S(2)}) %collective-permute-start.15) | collective-permute-done | bytes 4128 | tf_op jit(solution)/shard_map/ppermute | solution.py:24
  59.9 0.8 fusion.118
  62.2 3.5 %all-to-all-start = ((f32[2,1,512]{2,1,0:T(1,128)}), f32[2,1,512]{2,1,0:T(1,128)S(1)}, u32[]{:S(2)}, u32[]{:S(2)}) async-start(f32[2,1,512]{2,1,0:T(1,128)} %reshape.164), calls=%async_computation | async-start | bytes 8192 | tf_op jit(solution)/shard_map/all_to_all | solution.py:82
  65.9 3.7 %all-to-all-done = f32[2,1,512]{2,1,0:T(1,128)S(1)} async-done(((f32[2,1,512]{2,1,0:T(1,128)}), f32[2,1,512]{2,1,0:T(1,128)S(1)}, u32[]{:S(2)}, u32[]{:S(2)}) %all-to-all-start) | async-done | bytes 4128 | tf_op jit(solution)/shard_map/all_to_all | solution.py:82
  71.6 27.9 %all-gather = f32[256,64]{1,0:T(8,128)S(1)} all-gather(f32[16,64]{1,0:T(8,128)S(1)} %fusion.64), channel_id=2, replica_groups=mesh['wide'=16,'narrow'=2] {'wide'}, dimensions={0}, use_global_device_ids=true | all-gather | bytes 69632 | tf_op jit(solution)/shard_map/all_gather | solution.py:95
  100.4 17.8 %all-gather.1 = f32[256,64]{1,0:T(8,128)S(1)} all-gather(f32[16,64]{1,0:T(8,128)S(1)} %fusion.62), channel_id=3, replica_groups=mesh['wide'=16,'narrow'=2] {'wide'}, dimensions={0}, use_global_device_ids=true | all-gather | bytes 69632 | tf_op jit(solution)/shard_map/all_gather | solution.py:98
  118.2 0.9 fusion.24
  (42 shorter events, 5.2 us)
Async XLA Ops:
  0.6 0.9 copy-start
  2.5 4.5 %collective-permute-start = (f32[2,1,64,128]{3,2,1,0:T(8,128)S(1)}, f32[2,1,64,128]{3,2,1,0:T(8,128)S(1)}, u32[]{:S(2)}, u32[]{:S(2)}) collective-permute-start(f32[2,1,64,128]{3,2,1,0:T(8,128)S(1)} %get-tuple-element.25), channel_id=1, source_target_pairs={{2,0},{4,2},{6,4},{8,6},{10,8},{12,10},{14,12},{16,14},{18,16},{20... | collective-permute-start | bytes 196616 | tf_op jit(solution)/shard_map/ppermute | solution.py:26
  3.8 11.5 %copy-start.1 = (f32[2,2,64,128]{3,2,1,0:T(8,128)S(1)}, f32[2,2,64,128]{3,2,1,0:T(8,128)}, u32[]{:S(2)}) copy-start(f32[2,2,64,128]{3,2,1,0:T(8,128)} %param.3) | copy-start | bytes 393220
  3.8 4.1 %collective-permute-start.1 = (f32[2,1,64,128]{3,2,1,0:T(8,128)S(1)}, f32[2,1,64,128]{3,2,1,0:T(8,128)S(1)}, u32[]{:S(2)}, u32[]{:S(2)}) collective-permute-start(f32[2,1,64,128]{3,2,1,0:T(8,128)S(1)} %get-tuple-element.24), channel_id=1, source_target_pairs={{0,2},{2,4},{4,6},{6,8},{8,10},{10,12},{12,14},{14,16},{16,18},{18... | collective-permute-start | bytes 196616 | tf_op jit(solution)/shard_map/ppermute | solution.py:24
  7.9 6.1 %collective-permute-start.2 = (f32[2,4,1,128]{3,2,1,0:T(1,128)S(1)}, f32[2,4,1,128]{3,2,1,0:T(1,128)S(1)}, u32[]{:S(2)}, u32[]{:S(2)}) collective-permute-start(f32[2,4,1,128]{3,2,1,0:T(1,128)S(1)} %get-tuple-element.16), channel_id=1, source_target_pairs={{1,0},{3,2},{5,4},{7,6},{9,8},{11,10},{13,12},{15,14},{17,16},{19,... | collective-permute-start | bytes 12296 | tf_op jit(solution)/shard_map/ppermute | solution.py:26
  9.2 6.2 %collective-permute-start.3 = (f32[2,4,1,128]{3,2,1,0:T(1,128)S(1)}, f32[2,4,1,128]{3,2,1,0:T(1,128)S(1)}, u32[]{:S(2)}, u32[]{:S(2)}) collective-permute-start(f32[2,4,1,128]{3,2,1,0:T(1,128)S(1)} %get-tuple-element.17), channel_id=1, source_target_pairs={{0,1},{2,3},{4,5},{6,7},{8,9},{10,11},{12,13},{14,15},{16,17},{18,... | collective-permute-start | bytes 12296 | tf_op jit(solution)/shard_map/ppermute | solution.py:24
  15.5 5.4 %collective-permute-start.4 = (f32[2,1,64,128]{3,2,1,0:T(8,128)S(1)}, f32[2,1,64,128]{3,2,1,0:T(8,128)S(1)}, u32[]{:S(2)}, u32[]{:S(2)}) collective-permute-start(f32[2,1,64,128]{3,2,1,0:T(8,128)S(1)} %get-tuple-element.23), channel_id=1, source_target_pairs={{2,0},{4,2},{6,4},{8,6},{10,8},{12,10},{14,12},{16,14},{18,16},{20... | collective-permute-start | bytes 196616 | tf_op jit(solution)/shard_map/ppermute | solution.py:26
  16.8 5.0 %collective-permute-start.5 = (f32[2,1,64,128]{3,2,1,0:T(8,128)S(1)}, f32[2,1,64,128]{3,2,1,0:T(8,128)S(1)}, u32[]{:S(2)}, u32[]{:S(2)}) collective-permute-start(f32[2,1,64,128]{3,2,1,0:T(8,128)S(1)} %get-tuple-element.22), channel_id=1, source_target_pairs={{0,2},{2,4},{4,6},{6,8},{8,10},{10,12},{12,14},{14,16},{16,18},{18... | collective-permute-start | bytes 196616 | tf_op jit(solution)/shard_map/ppermute | solution.py:24
  21.8 5.8 %collective-permute-start.6 = (f32[2,4,1,128]{3,2,1,0:T(1,128)S(1)}, f32[2,4,1,128]{3,2,1,0:T(1,128)S(1)}, u32[]{:S(2)}, u32[]{:S(2)}) collective-permute-start(f32[2,4,1,128]{3,2,1,0:T(1,128)S(1)} %get-tuple-element.14), channel_id=1, source_target_pairs={{1,0},{3,2},{5,4},{7,6},{9,8},{11,10},{13,12},{15,14},{17,16},{19,... | collective-permute-start | bytes 12296 | tf_op jit(solution)/shard_map/ppermute | solution.py:26
  23.1 5.9 %collective-permute-start.7 = (f32[2,4,1,128]{3,2,1,0:T(1,128)S(1)}, f32[2,4,1,128]{3,2,1,0:T(1,128)S(1)}, u32[]{:S(2)}, u32[]{:S(2)}) collective-permute-start(f32[2,4,1,128]{3,2,1,0:T(1,128)S(1)} %get-tuple-element.15), channel_id=1, source_target_pairs={{0,1},{2,3},{4,5},{6,7},{8,9},{10,11},{12,13},{14,15},{16,17},{18,... | collective-permute-start | bytes 12296 | tf_op jit(solution)/shard_map/ppermute | solution.py:24
  29.2 7.1 %collective-permute-start.8 = (f32[2,1,64,128]{3,2,1,0:T(8,128)S(1)}, f32[2,1,64,128]{3,2,1,0:T(8,128)S(1)}, u32[]{:S(2)}, u32[]{:S(2)}) collective-permute-start(f32[2,1,64,128]{3,2,1,0:T(8,128)S(1)} %get-tuple-element.21), channel_id=1, source_target_pairs={{2,0},{4,2},{6,4},{8,6},{10,8},{12,10},{14,12},{16,14},{18,16},{20... | collective-permute-start | bytes 196616 | tf_op jit(solution)/shard_map/ppermute | solution.py:26
  30.5 6.7 %collective-permute-start.9 = (f32[2,1,64,128]{3,2,1,0:T(8,128)S(1)}, f32[2,1,64,128]{3,2,1,0:T(8,128)S(1)}, u32[]{:S(2)}, u32[]{:S(2)}) collective-permute-start(f32[2,1,64,128]{3,2,1,0:T(8,128)S(1)} %get-tuple-element.20), channel_id=1, source_target_pairs={{0,2},{2,4},{4,6},{6,8},{8,10},{10,12},{12,14},{14,16},{16,18},{18... | collective-permute-start | bytes 196616 | tf_op jit(solution)/shard_map/ppermute | solution.py:24
  37.2 5.9 %collective-permute-start.10 = (f32[2,4,1,128]{3,2,1,0:T(1,128)S(1)}, f32[2,4,1,128]{3,2,1,0:T(1,128)S(1)}, u32[]{:S(2)}, u32[]{:S(2)}) collective-permute-start(f32[2,4,1,128]{3,2,1,0:T(1,128)S(1)} %get-tuple-element.12), channel_id=1, source_target_pairs={{1,0},{3,2},{5,4},{7,6},{9,8},{11,10},{13,12},{15,14},{17,16},{19,... | collective-permute-start | bytes 12296 | tf_op jit(solution)/shard_map/ppermute | solution.py:26
  38.5 5.9 %collective-permute-start.11 = (f32[2,4,1,128]{3,2,1,0:T(1,128)S(1)}, f32[2,4,1,128]{3,2,1,0:T(1,128)S(1)}, u32[]{:S(2)}, u32[]{:S(2)}) collective-permute-start(f32[2,4,1,128]{3,2,1,0:T(1,128)S(1)} %get-tuple-element.13), channel_id=1, source_target_pairs={{0,1},{2,3},{4,5},{6,7},{8,9},{10,11},{12,13},{14,15},{16,17},{18,... | collective-permute-start | bytes 12296 | tf_op jit(solution)/shard_map/ppermute | solution.py:24
  44.5 7.4 %collective-permute-start.12 = (f32[2,1,64,128]{3,2,1,0:T(8,128)S(1)}, f32[2,1,64,128]{3,2,1,0:T(8,128)S(1)}, u32[]{:S(2)}, u32[]{:S(2)}) collective-permute-start(f32[2,1,64,128]{3,2,1,0:T(8,128)S(1)} %get-tuple-element.19), channel_id=1, source_target_pairs={{2,0},{4,2},{6,4},{8,6},{10,8},{12,10},{14,12},{16,14},{18,16},{20... | collective-permute-start | bytes 196616 | tf_op jit(solution)/shard_map/ppermute | solution.py:26
  45.8 6.9 %collective-permute-start.13 = (f32[2,1,64,128]{3,2,1,0:T(8,128)S(1)}, f32[2,1,64,128]{3,2,1,0:T(8,128)S(1)}, u32[]{:S(2)}, u32[]{:S(2)}) collective-permute-start(f32[2,1,64,128]{3,2,1,0:T(8,128)S(1)} %get-tuple-element.18), channel_id=1, source_target_pairs={{0,2},{2,4},{4,6},{6,8},{8,10},{10,12},{12,14},{14,16},{16,18},{18... | collective-permute-start | bytes 196616 | tf_op jit(solution)/shard_map/ppermute | solution.py:24
  52.7 5.9 %collective-permute-start.14 = (f32[2,4,1,128]{3,2,1,0:T(1,128)S(1)}, f32[2,4,1,128]{3,2,1,0:T(1,128)S(1)}, u32[]{:S(2)}, u32[]{:S(2)}) collective-permute-start(f32[2,4,1,128]{3,2,1,0:T(1,128)S(1)} %get-tuple-element.10), channel_id=1, source_target_pairs={{1,0},{3,2},{5,4},{7,6},{9,8},{11,10},{13,12},{15,14},{17,16},{19,... | collective-permute-start | bytes 12296 | tf_op jit(solution)/shard_map/ppermute | solution.py:26
  54.0 5.9 %collective-permute-start.15 = (f32[2,4,1,128]{3,2,1,0:T(1,128)S(1)}, f32[2,4,1,128]{3,2,1,0:T(1,128)S(1)}, u32[]{:S(2)}, u32[]{:S(2)}) collective-permute-start(f32[2,4,1,128]{3,2,1,0:T(1,128)S(1)} %get-tuple-element.11), channel_id=1, source_target_pairs={{0,1},{2,3},{4,5},{6,7},{8,9},{10,11},{12,13},{14,15},{16,17},{18,... | collective-permute-start | bytes 12296 | tf_op jit(solution)/shard_map/ppermute | solution.py:24
  62.2 7.3 %all-to-all-start = ((f32[2,1,512]{2,1,0:T(1,128)}), f32[2,1,512]{2,1,0:T(1,128)S(1)}, u32[]{:S(2)}, u32[]{:S(2)}) async-start(f32[2,1,512]{2,1,0:T(1,128)} %reshape.164), calls=%async_computation | async-start | bytes 8192 | tf_op jit(solution)/shard_map/all_to_all | solution.py:82
where the time goes:
time: 120 us; the launch traced here: 119 us
  starting transfers between devices  51.4 us (43%)
  blocking collectives  45.7 us (38%)
  waiting for transfers between devices  12.3 us (10%)
  other arithmetic  4.09 us (3%)
  matrix products  2.44 us (2%)
  local copies, waits for them, and re-layouts  2.1 us (2%)
    ppermute x8, starting transfers between devices, with_halo(): lax.ppermute(tail, axis, [(i, (i + 1) % count) for i in range(ends)])  37.6 us
    all_gather x1, blocking collectives, body(): modes = accumulate(lax.all_gather(spectrum, 'wide', axis=0, tiled=True))  27.9 us
    all_gather x1, blocking collectives, body(): lax.all_gather(back, 'wide', axis=0, tiled=True)  17.8 us
    ppermute x8, starting transfers between devices, with_halo(): lax.ppermute(head, axis, [((i + 1) % count, i) for i in range(ends)])  10.3 us
    ppermute x8, waiting for transfers between devices, with_halo(): lax.ppermute(tail, axis, [(i, (i + 1) % count) for i in range(ends)])  8.62 us
    all_to_all x1, waiting for transfers between devices, body(): lax.all_to_all(coarse, 'narrow', split_axis=1, concat_axis=3, tiled=True)  3.66 us
    all_to_all x1, starting transfers between devices, body(): lax.all_to_all(coarse, 'narrow', split_axis=1, concat_axis=3, tiled=True)  3.55 us
  transfers between devices with their start and end apart: 17, of which 9 were waited for; matrix products, arithmetic and copies ran while one was open for 0% of the time, Pallas kernels for 0%

commit v1 on v0

v1 whole, which is shorter than its diff:
```python
import functools

import jax
import jax.numpy as jnp
import numpy as np
from jax import lax
from jax.experimental import pallas as pl
from jax.experimental.pallas import tpu as pltpu
from jax.sharding import PartitionSpec as P

SWEEPS = 4
OMEGA = 0.8
COEF_X = 1.0
COEF_Y = 1.0
COEF_Z = 4.0
SHIFT = 0.02
MESH = pl.DeviceIdType.MESH
LANES = 128


def sine(count):
    index = np.arange(count, dtype=np.int64) + 1
    product = index[:, None] * index[None, :] % (2 * (count + 1))
    return np.sqrt(2.0 / (count + 1)) * np.sin(np.pi * product / (count + 1))


def eigen(count):
    return 2.0 - 2.0 * np.cos(np.pi * (np.arange(count) + 1) / (count + 1))


def tables(dirs, cells_y, cells_z, narrow, coarse_x, coarse_y, coarse_z):
    part = LANES // coarse_y
    rows = coarse_z // part
    s_y, s_z = sine(coarse_y), sine(coarse_z)
    lift = np.repeat(s_z, cells_z // coarse_z, axis=0).T
    fine = np.repeat(s_y, 2, axis=0).reshape(narrow, cells_y, coarse_y)
    spread = np.zeros((narrow, dirs, dirs, cells_y, part, coarse_y))
    for d in range(dirs):
        spread[:, d, d] = fine[:, :, None, :]
    spread = spread.reshape(narrow, dirs, dirs * cells_y, LANES)
    plane = COEF_Y * eigen(coarse_y)[None, :] + COEF_Z * eigen(coarse_z)[:, None] + SHIFT
    plane = plane.reshape(part, rows, coarse_y).transpose(1, 0, 2).reshape(rows, LANES)
    steps = np.arange(2 * coarse_x + 1)
    wave = np.cos(np.pi * (np.outer(steps, np.arange(coarse_x) + 1) % (2 * coarse_x + 2)) / (coarse_x + 1))
    inverse = 1.0 / (COEF_X * eigen(coarse_x)[:, None] + plane.reshape(1, -1))
    green = (wave @ inverse / (coarse_x + 1)).reshape(-1, rows, LANES)
    mix = np.zeros((part * coarse_z, LANES))
    mix[:, :rows] = s_z.reshape(coarse_z, part, rows).transpose(1, 0, 2).reshape(part * coarse_z, rows)
    back = np.zeros((LANES, LANES))
    back[:, :coarse_y] = np.tile(s_y, (part, 1))
    return [np.asarray(t, np.float32) for t in (lift, spread, green, mix, back)]


def dot(a, b, dims=((1,), (0,))):
    return lax.dot_general(
        a, b, (dims, ((), ())), precision=lax.Precision.HIGHEST, preferred_element_type=jnp.float32
    )


def kernel(
    wide, narrow, cot, obs, sig, lift_h, spread_h, green_h, mix_h, back_h, grad, coarse,
    cc, ww, hx, hy, ys, lift, spread, green, mix, back, pack, recv,
    tsem, sx, rx, sy, ry, sc, rc,
):
    dirs, cells_x, cells_y, cells_z = cot.shape
    last = cells_x - 1
    w = lax.axis_index("wide")
    n = lax.axis_index("narrow")
    total = wide * narrow
    me = w * narrow + n

    barrier = pltpu.get_barrier_semaphore()

    def greet(k, carry):
        peer = lax.rem(me + k, total)
        pl.semaphore_signal(
            barrier, inc=1, device_id=(lax.div(peer, narrow), lax.rem(peer, narrow)), device_id_type=MESH
        )
        return carry

    lax.fori_loop(1, total, greet, 0)

    loads = [
        pltpu.make_async_copy(src, dst, tsem.at[i])
        for i, (src, dst) in enumerate(
            ((lift_h, lift), (spread_h.at[n], spread), (green_h, green), (mix_h, mix), (back_h, back))
        )
    ]
    for load in loads:
        load.start()

    edges = (w > 0, w < wide - 1)
    sides = (n > 0, n < narrow - 1)
    for s in range(2):

        @pl.when(jnp.logical_not(edges[s]))
        def _():
            for sweep in range(SWEEPS):
                hx[sweep, s] = jnp.zeros(hx.shape[2:], jnp.float32)

        @pl.when(jnp.logical_not(sides[s]))
        def _():
            for sweep in range(SWEEPS):
                hy[sweep, s] = jnp.zeros(hy.shape[2:], jnp.float32)

    for x in range(cells_x):
        share = OMEGA / (6.0 + sig[x])
        for d in range(dirs):
            fluid = obs[d, x].astype(jnp.float32)
            cc[x, d] = share * fluid
            grad[d, x] = cot[d, x]

    def wide_copy(sweep, s):
        return pltpu.make_async_remote_copy(
            src_ref=ww.at[sweep, 0 if s == 0 else last],
            dst_ref=hx.at[sweep, 1 - s],
            send_sem=sx.at[sweep, s],
            recv_sem=rx.at[sweep, 1 - s],
            device_id=(w - 1 if s == 0 else w + 1, n),
            device_id_type=MESH,
        )

    def wide_arrival(sweep, s):
        return pltpu.make_async_copy(hx.at[sweep, s], hx.at[sweep, s], rx.at[sweep, s])

    def narrow_copy(sweep, s):
        return pltpu.make_async_remote_copy(
            src_ref=ys.at[sweep, s],
            dst_ref=hy.at[sweep, 1 - s],
            send_sem=sy.at[sweep, s],
            recv_sem=ry.at[sweep, 1 - s],
            device_id=(w, n - 1 if s == 0 else n + 1),
            device_id_type=MESH,
        )

    def narrow_arrival(sweep, s):
        return pltpu.make_async_copy(hy.at[sweep, s], hy.at[sweep, s], ry.at[sweep, s])

    lane = lax.broadcasted_iota(jnp.int32, (cells_y, cells_z), 1)
    row = lax.broadcasted_iota(jnp.int32, (cells_y, cells_z), 0)
    for sweep in range(SWEEPS):
        for x in range(cells_x):
            for d in range(dirs):
                value = cc[x, d] * grad[d, x]
                ww[sweep, x, d] = value
                ys[sweep, 0, x * dirs + d] = value[0]
                ys[sweep, 1, x * dirs + d] = value[cells_y - 1]
        if sweep == 0:
            pl.semaphore_wait(barrier, total - 1)
        for s in range(2):

            @pl.when(edges[s])
            def _():
                wide_copy(sweep, s).start()

            @pl.when(sides[s])
            def _():
                narrow_copy(sweep, s).start()

        for x in range(cells_x):
            for d in range(dirs):
                here = ww[sweep, x, d]
                keep = jnp.where(cc[x, d] > 0.0, 1.0 - OMEGA, 1.0)
                near = grad[d, x] * keep
                near += jnp.where(lane == 0, 0.0, pltpu.roll(here, 1, 1))
                near += jnp.where(lane == cells_z - 1, 0.0, pltpu.roll(here, cells_z - 1, 1))
                near += jnp.where(row == 0, 0.0, pltpu.roll(here, 1, 0))
                near += jnp.where(row == cells_y - 1, 0.0, pltpu.roll(here, cells_y - 1, 0))
                if x > 0:
                    near += ww[sweep, x - 1, d]
                if x < last:
                    near += ww[sweep, x + 1, d]
                grad[d, x] = near
        for s in range(2):

            @pl.when(sides[s])
            def _():
                narrow_arrival(sweep, s).wait()

        for x in range(cells_x):
            for d in range(dirs):
                r = x * dirs + d
                grad[d, x, 0:1] += hy[sweep, 0, r : r + 1]
                grad[d, x, cells_y - 1 : cells_y] += hy[sweep, 1, r : r + 1]
        for s in range(2):

            @pl.when(edges[s])
            def _():
                wide_arrival(sweep, s).wait()

            for d in range(dirs):
                grad[d, 0 if s == 0 else last] += hx[sweep, s, d]

    for load in loads:
        load.wait()
    rows = recv.shape[1]
    slab = jnp.concatenate([sum(grad[d, x] for x in range(cells_x)) for d in range(dirs)], axis=0)
    modes = dot(lift[...], slab, ((1,), (1,)))
    part = lift.shape[0] // rows
    width = LANES // part
    column = lax.broadcasted_iota(jnp.int32, (rows, LANES), 1)
    for d in range(dirs):
        wave = dot(modes, spread[d])
        packed = wave[0:rows]
        for h in range(1, part):
            packed = jnp.where(column < h * width, packed, wave[h * rows : (h + 1) * rows])
        pack[d] = packed

    def send(k, carry):
        peer = lax.rem(me + k, total)
        other = lax.rem(peer, narrow)
        for d in range(dirs // narrow):
            pltpu.make_async_remote_copy(
                src_ref=pack.at[other],
                dst_ref=recv.at[me],
                send_sem=sc,
                recv_sem=rc,
                device_id=(lax.div(peer, narrow), other),
                device_id_type=MESH,
            ).start()
        return carry

    lax.fori_loop(1, total, send, 0)
    recv[me] = pack[n]
    all_but_one = recv.at[pl.ds(0, total - 1)]
    pltpu.make_async_copy(all_but_one, all_but_one, rc).wait()

    def solve(x, carry):
        near = green[lax.abs(w - x)] - green[w + x + 2]
        field = recv[x * narrow]
        for m in range(1, narrow):
            field += recv[x * narrow + m]
        return carry + near * field

    solved = lax.fori_loop(0, wide, solve, jnp.zeros((rows, LANES), jnp.float32), unroll=min(wide, 16))
    wave = dot(mix[:, 0:rows], solved)
    count_z = coarse.shape[2]
    column = lax.broadcasted_iota(jnp.int32, (count_z, LANES), 1)
    both = wave[0:count_z]
    for h in range(1, part):
        both = jnp.where(column < h * width, both, wave[h * count_z : (h + 1) * count_z])
    coarse[0, 0] = dot(both, back[...])[:, 0 : coarse.shape[3]]

    for sweep in range(SWEEPS):
        for s in range(2):

            @pl.when(edges[s])
            def _():
                wide_copy(sweep, s).wait_send()

            @pl.when(sides[s])
            def _():
                narrow_copy(sweep, s).wait_send()

    pltpu.make_async_copy(all_but_one, all_but_one, sc).wait()


def body(wide, narrow, fine_cot, obstacle, sigma):
    dirs, cells_x, cells_y, cells_z = fine_cot.shape
    coarse_x, coarse_y, coarse_z = wide * cells_x // 2, narrow * cells_y // 2, cells_z // 8
    made = tables(dirs, cells_y, cells_z, narrow, coarse_x, coarse_y, coarse_z)
    lift, spread, green, mix, back = made
    total = wide * narrow
    rows = green.shape[1]
    f32 = jnp.float32
    vmem = pl.BlockSpec(memory_space=pltpu.VMEM)
    anywhere = pl.BlockSpec(memory_space=pl.ANY)
    plane = (cells_y, cells_z)
    return pl.pallas_call(
        functools.partial(kernel, wide, narrow),
        out_shape=(
            jax.ShapeDtypeStruct(fine_cot.shape, f32),
            jax.ShapeDtypeStruct((1, 1, coarse_z, coarse_y), f32),
        ),
        in_specs=[vmem] * 3 + [anywhere] * 5,
        out_specs=(vmem, vmem),
        scratch_shapes=[
            pltpu.VMEM((cells_x, dirs) + plane, f32),
            pltpu.VMEM((SWEEPS, cells_x, dirs) + plane, f32),
            pltpu.VMEM((SWEEPS, 2, dirs) + plane, f32),
            pltpu.VMEM((SWEEPS, 2, cells_x * dirs, cells_z), f32),
            pltpu.VMEM((SWEEPS, 2, cells_x * dirs, cells_z), f32),
            pltpu.VMEM(lift.shape, f32),
            pltpu.VMEM(spread.shape[1:], f32),
            pltpu.VMEM(green.shape, f32),
            pltpu.VMEM(mix.shape, f32),
            pltpu.VMEM(back.shape, f32),
            pltpu.VMEM((dirs, rows, LANES), f32),
            pltpu.VMEM((total, rows, LANES), f32),
            pltpu.SemaphoreType.DMA((5,)),
            pltpu.SemaphoreType.DMA((SWEEPS, 2)),
            pltpu.SemaphoreType.DMA((SWEEPS, 2)),
            pltpu.SemaphoreType.DMA((SWEEPS, 2)),
            pltpu.SemaphoreType.DMA((SWEEPS, 2)),
            pltpu.SemaphoreType.DMA,
            pltpu.SemaphoreType.DMA,
        ],
        compiler_params=pltpu.CompilerParams(
            collective_id=0, has_side_effects=True, vmem_limit_bytes=40 * 2**20
        ),
    )(fine_cot, obstacle, sigma, *made)


def solution(mesh):
    placed = (
        P(None, "wide", "narrow", None),
        P(None, "wide", "narrow", None),
        P("wide", "narrow", None),
    )
    return jax.shard_map(
        functools.partial(body, mesh.shape["wide"], mesh.shape["narrow"]),
        mesh=mesh,
        in_specs=placed,
        out_specs=(P(None, "wide", "narrow", None), P("wide", "narrow", None, None)),
        check_vma=False,
    )
```

time: 120 us -> 33.6 us (0.28)
  starting transfers between devices: 51.4 us -> 0 us
  blocking collectives: 45.7 us -> 0 us
  Pallas kernels: 0 us -> 24.5 us
  waiting for transfers between devices: 12.3 us -> 0 us
  local copies, waits for them, and re-layouts: 2.1 us -> 8.01 us
  other arithmetic: 4.09 us -> 0 us
  matrix products: 2.44 us -> 0 us
    ppermute x16 -> x0, starting transfers between devices: 47.9 us -> none  [the longest x8 37.6 us: with_halo(): lax.ppermute(tail, axis, [(i, (i + 1) % count) for i in range(ends)])]
    all_gather x2 -> x0, blocking collectives: 45.7 us -> none  [the longest x1 27.9 us: body(): modes = accumulate(lax.all_gather(spectrum, 'wide', axis=0, tiled=True))]
    pallas_call x0 -> x1, Pallas kernels: none -> 24.5 us  [body(): pl.pallas_call(functools.partial(kernel, wide, narrow), out_shape=(jax.Sh...]
    ppermute x16 -> x0, waiting for transfers between devices: 8.64 us -> none  [the longest x8 8.62 us: with_halo(): lax.ppermute(tail, axis, [(i, (i + 1) % count) for i in range(ends)])]
    unnamed x6 -> x18, local copies, waits for them, and re-layouts: 0.81 us -> 8.01 us
    all_to_all x1 -> x0, waiting for transfers between devices: 3.66 us -> none  [body(): lax.all_to_all(coarse, 'narrow', split_axis=1, concat_axis=3, tiled=True)]
    all_to_all x1 -> x0, starting transfers between devices: 3.55 us -> none  [body(): lax.all_to_all(coarse, 'narrow', split_axis=1, concat_axis=3, tiled=True)]
    dot_general x6 -> x0, matrix products: 2.44 us -> none  [the longest x2 1.11 us: accumulate(): return jnp.einsum('kx,xdwv->kdwv', table, piece, precision=high)]
  transfers between devices with their start and end apart: 17 -> 0, of which waited for: 9 -> 0; matrix products, arithmetic and copies ran while one was open for 0% -> 0% of each run, Pallas kernels for 0% -> 0%
where the time goes in v1:
time: 33.6 us; the launch traced here: 33.2 us
  Pallas kernels  24.5 us (73%)
  local copies, waits for them, and re-layouts  8.01 us (24%)
  between operations  0.65 us (2%)
    pallas_call x1, Pallas kernels, body(): pl.pallas_call(functools.partial(kernel, wide, narrow), out_shape=(jax.Sh...  24.5 us
    unnamed x18, local copies, waits for them, and re-layouts  8.01 us

profile of v1, /device:TPU:0, one launch (start us, length us, event | category | flops | bytes accessed | tf_op | source)
XLA Modules:
  0.0 33.2 jit_solution(9384603558956524372)
XLA Ops:
  0.6 0.0 copy-start
  0.6 0.9 %copy-done = f32[2,2,128,128]{3,2,1,0:T(8,128)S(1)} copy-done((f32[2,2,128,128]{3,2,1,0:T(8,128)S(1)}, f32[2,2,128,128]{3,2,1,0:T(8,128)}, u32[]{:S(2)}) %copy-start) | copy-done | bytes 262168
  1.6 0.0 copy-start.1
  1.6 0.9 %copy-done.1 = f32[33,8,128]{2,1,0:T(8,128)S(1)} copy-done((f32[33,8,128]{2,1,0:T(8,128)S(1)}, f32[33,8,128]{2,1,0:T(8,128)}, u32[]{:S(2)}) %copy-start.1) | copy-done | bytes 135192
  2.5 0.0 copy-start.2
  2.5 0.9 %copy-done.2 = f32[2,2,64,128]{3,2,1,0:T(8,128)S(1)} copy-done((f32[2,2,64,128]{3,2,1,0:T(8,128)S(1)}, f32[2,2,64,128]{3,2,1,0:T(8,128)}, u32[]{:S(2)}) %copy-start.2) | copy-done | bytes 131096
  3.4 0.0 copy-start.3
  3.4 0.9 %copy-done.3 = s32[2,2,64,128]{3,2,1,0:T(8,128)S(1)} copy-done((s32[2,2,64,128]{3,2,1,0:T(8,128)S(1)}, s32[2,2,64,128]{3,2,1,0:T(8,128)}, u32[]{:S(2)}) %copy-start.3) | copy-done | bytes 131096
  4.3 0.0 copy-start.4
  4.3 0.8 %copy-done.4 = f32[2,64,128]{2,1,0:T(8,128)S(1)} copy-done((f32[2,64,128]{2,1,0:T(8,128)S(1)}, f32[2,64,128]{2,1,0:T(8,128)}, u32[]{:S(2)}) %copy-start.4) | copy-done | bytes 65560
  5.1 0.0 copy-start.5
  5.1 0.8 %copy-done.5 = f32[128,128]{1,0:T(8,128)S(1)} copy-done((f32[128,128]{1,0:T(8,128)S(1)}, f32[128,128]{1,0:T(8,128)}, u32[]{:S(2)}) %copy-start.5) | copy-done | bytes 65560
  6.0 0.0 copy-start.6
  6.0 0.7 %copy-done.6 = f32[32,128]{1,0:T(8,128)S(1)} copy-done((f32[32,128]{1,0:T(8,128)S(1)}, f32[32,128]{1,0:T(8,128)}, u32[]{:S(2)}) %copy-start.6) | copy-done | bytes 16408
  6.7 0.0 copy-start.7
  6.7 0.7 %copy-done.7 = f32[16,128]{1,0:T(8,128)S(1)} copy-done((f32[16,128]{1,0:T(8,128)S(1)}, f32[16,128]{1,0:T(8,128)}, u32[]{:S(2)}) %copy-start.7) | copy-done | bytes 8216
  7.4 24.5 %shard_map.95 = (f32[2,2,64,128]{3,2,1,0:T(8,128)S(1)}, f32[1,1,16,64]{3,2,1,0:T(8,128)S(1)}) custom-call(f32[2,2,64,128]{3,2,1,0:T(8,128)S(1)} %copy-done.2, s32[2,2,64,128]{3,2,1,0:T(8,128)S(1)} %copy-done.3, f32[2,64,128]{2,1,0:T(8,128)S(1)} %copy-done.4, f32[16,128]{1,0:T(8,128)S(1)} %copy-done.7, f32[2,2,128,128]{3,2,1,0:T(8,128)S(1)} %copy-done, ...), custom_call_target="tpu_custom_call" | custom-call | tf_op jit(solution)/shard_map/pallas_call | solution.py:269
  31.9 0.7 %copy.12 = f32[2,2,64,128]{3,2,1,0:T(8,128)} copy(f32[2,2,64,128]{3,2,1,0:T(8,128)S(1)} %get-tuple-element.4) | data formatting | bytes 262144
  32.6 0.6 %copy.13 = f32[1,1,16,64]{3,2,1,0:T(8,128)} copy(f32[1,1,16,64]{3,2,1,0:T(8,128)S(1)} %get-tuple-element.5) | data formatting | bytes 8192
Async XLA Ops:
  0.6 1.0 %copy-start = (f32[2,2,128,128]{3,2,1,0:T(8,128)S(1)}, f32[2,2,128,128]{3,2,1,0:T(8,128)}, u32[]{:S(2)}) copy-start(f32[2,2,128,128]{3,2,1,0:T(8,128)} %constant.11.clone.spread_h) | copy-start | bytes 786436
  1.6 0.9 %copy-start.1 = (f32[33,8,128]{2,1,0:T(8,128)S(1)}, f32[33,8,128]{2,1,0:T(8,128)}, u32[]{:S(2)}) copy-start(f32[33,8,128]{2,1,0:T(8,128)} %constant.12.clone.green_h) | copy-start | bytes 405508
  2.5 0.9 %copy-start.2 = (f32[2,2,64,128]{3,2,1,0:T(8,128)S(1)}, f32[2,2,64,128]{3,2,1,0:T(8,128)}, u32[]{:S(2)}) copy-start(f32[2,2,64,128]{3,2,1,0:T(8,128)} %cot.1) | copy-start | bytes 393220
  3.4 0.9 %copy-start.3 = (s32[2,2,64,128]{3,2,1,0:T(8,128)S(1)}, s32[2,2,64,128]{3,2,1,0:T(8,128)}, u32[]{:S(2)}) copy-start(s32[2,2,64,128]{3,2,1,0:T(8,128)} %obs.1) | copy-start | bytes 393220
  4.3 0.8 %copy-start.4 = (f32[2,64,128]{2,1,0:T(8,128)S(1)}, f32[2,64,128]{2,1,0:T(8,128)}, u32[]{:S(2)}) copy-start(f32[2,64,128]{2,1,0:T(8,128)} %sig.1) | copy-start | bytes 196612
  5.1 0.8 %copy-start.5 = (f32[128,128]{1,0:T(8,128)S(1)}, f32[128,128]{1,0:T(8,128)}, u32[]{:S(2)}) copy-start(f32[128,128]{1,0:T(8,128)} %constant.14.clone.back_h) | copy-start | bytes 196612
  6.0 0.7 %copy-start.6 = (f32[32,128]{1,0:T(8,128)S(1)}, f32[32,128]{1,0:T(8,128)}, u32[]{:S(2)}) copy-start(f32[32,128]{1,0:T(8,128)} %constant.13.clone.mix_h) | copy-start | bytes 49156
  6.7 0.7 %copy-start.7 = (f32[16,128]{1,0:T(8,128)S(1)}, f32[16,128]{1,0:T(8,128)}, u32[]{:S(2)}) copy-start(f32[16,128]{1,0:T(8,128)} %constant.10.clone.lift_h) | copy-start | bytes 24580

commit v2 on v1

--- a/solution.py
+++ b/solution.py
@@ -58,16 +58,34 @@
 
 
 def kernel(
-    wide, narrow, cot, obs, sig, lift_h, spread_h, green_h, mix_h, back_h, grad, coarse,
-    cc, ww, hx, hy, ys, lift, spread, green, mix, back, pack, recv,
+    wide, narrow, cot_h, obs_h, sig_h, lift_h, spread_h, green_h, mix_h, back_h, grad, coarse,
+    obs, sig, cc, ww, hx, hy, ys, lift, spread, green, mix, back, pack, recv,
     tsem, sx, rx, sy, ry, sc, rc,
 ):
-    dirs, cells_x, cells_y, cells_z = cot.shape
+    dirs, cells_x, cells_y, cells_z = grad.shape
     last = cells_x - 1
     w = lax.axis_index("wide")
     n = lax.axis_index("narrow")
     total = wide * narrow
     me = w * narrow + n
+
+    loads = [
+        pltpu.make_async_copy(src, dst, tsem.at[i])
+        for i, (src, dst) in enumerate(
+            (
+                (sig_h, sig),
+                (obs_h, obs),
+                (cot_h, grad),
+                (lift_h, lift),
+                (spread_h.at[n], spread),
+                (green_h, green),
+                (mix_h, mix),
+                (back_h, back),
+            )
+        )
+    ]
+    for load in loads:
+        load.start()
 
     barrier = pltpu.get_barrier_semaphore()
 
@@ -80,15 +98,6 @@
 
     lax.fori_loop(1, total, greet, 0)
 
-    loads = [
-        pltpu.make_async_copy(src, dst, tsem.at[i])
-        for i, (src, dst) in enumerate(
-            ((lift_h, lift), (spread_h.at[n], spread), (green_h, green), (mix_h, mix), (back_h, back))
-        )
-    ]
-    for load in loads:
-        load.start()
-
     edges = (w > 0, w < wide - 1)
     sides = (n > 0, n < narrow - 1)
     for s in range(2):
@@ -103,12 +112,13 @@
             for sweep in range(SWEEPS):
                 hy[sweep, s] = jnp.zeros(hy.shape[2:], jnp.float32)
 
+    for load in loads[:3]:
+        load.wait()
     for x in range(cells_x):
         share = OMEGA / (6.0 + sig[x])
         for d in range(dirs):
             fluid = obs[d, x].astype(jnp.float32)
             cc[x, d] = share * fluid
-            grad[d, x] = cot[d, x]
 
     def wide_copy(sweep, s):
         return pltpu.make_async_remote_copy(
@@ -191,7 +201,7 @@
             for d in range(dirs):
                 grad[d, 0 if s == 0 else last] += hx[sweep, s, d]
 
-    for load in loads:
+    for load in loads[3:]:
         load.wait()
     rows = recv.shape[1]
     slab = jnp.concatenate([sum(grad[d, x] for x in range(cells_x)) for d in range(dirs)], axis=0)
@@ -264,7 +274,7 @@
     rows = green.shape[1]
     f32 = jnp.float32
     vmem = pl.BlockSpec(memory_space=pltpu.VMEM)
-    anywhere = pl.BlockSpec(memory_space=pl.ANY)
+    stay = pl.BlockSpec(memory_space=pl.ANY)
     plane = (cells_y, cells_z)
     return pl.pallas_call(
         functools.partial(kernel, wide, narrow),
@@ -272,9 +282,11 @@
             jax.ShapeDtypeStruct(fine_cot.shape, f32),
             jax.ShapeDtypeStruct((1, 1, coarse_z, coarse_y), f32),
         ),
-        in_specs=[vmem] * 3 + [anywhere] * 5,
+        in_specs=[stay] * 8,
         out_specs=(vmem, vmem),
         scratch_shapes=[
+            pltpu.VMEM(obstacle.shape, obstacle.dtype),
+            pltpu.VMEM(sigma.shape, f32),
             pltpu.VMEM((cells_x, dirs) + plane, f32),
             pltpu.VMEM((SWEEPS, cells_x, dirs) + plane, f32),
             pltpu.VMEM((SWEEPS, 2, dirs) + plane, f32),
@@ -287,7 +299,7 @@
             pltpu.VMEM(back.shape, f32),
             pltpu.VMEM((dirs, rows, LANES), f32),
             pltpu.VMEM((total, rows, LANES), f32),
-            pltpu.SemaphoreType.DMA((5,)),
+            pltpu.SemaphoreType.DMA((8,)),
             pltpu.SemaphoreType.DMA((SWEEPS, 2)),
             pltpu.SemaphoreType.DMA((SWEEPS, 2)),
             pltpu.SemaphoreType.DMA((SWEEPS, 2)),
@@ -296,7 +308,7 @@
             pltpu.SemaphoreType.DMA,
         ],
         compiler_params=pltpu.CompilerParams(
-            collective_id=0, has_side_effects=True, vmem_limit_bytes=40 * 2**20
+            collective_id=0, has_side_effects=True, vmem_limit_bytes=60 * 2**20
         ),
     )(fine_cot, obstacle, sigma, *made)
 

time: 33.6 us -> 28.3 us (0.84)
  local copies, waits for them, and re-layouts: 8.01 us -> 2.18 us
  Pallas kernels: 24.5 us -> 25.3 us
    unnamed x18 -> x4, local copies, waits for them, and re-layouts: 8.01 us -> 2.18 us
    pallas_call x1, Pallas kernels: 24.5 us -> 25.3 us  [body(): pl.pallas_call(functools.partial(kernel, wide, narrow), out_shape=(jax.Sh...]
where the time goes in v2:
time: 28.3 us; the launch traced here: 28.2 us
  Pallas kernels  25.3 us (89%)
  local copies, waits for them, and re-layouts  2.18 us (8%)
  between operations  0.65 us (2%)
    pallas_call x1, Pallas kernels, body(): pl.pallas_call(functools.partial(kernel, wide, narrow), out_shape=(jax.Sh...  25.3 us
    unnamed x4, local copies, waits for them, and re-layouts  2.18 us

profile of v2, /device:TPU:0, one launch (start us, length us, event | category | flops | bytes accessed | tf_op | source)
XLA Modules:
  0.0 28.2 jit_solution(6799863736959054099)
XLA Ops:
  0.6 25.3 %shard_map.95 = (f32[2,2,64,128]{3,2,1,0:T(8,128)}, f32[1,1,16,64]{3,2,1,0:T(8,128)}) custom-call(f32[2,2,64,128]{3,2,1,0:T(8,128)} %cot_h.1, s32[2,2,64,128]{3,2,1,0:T(8,128)} %obs_h.1, f32[2,64,128]{2,1,0:T(8,128)} %sig_h.1, f32[16,128]{1,0:T(8,128)} %constant.10.clone.lift_h, f32[2,2,128,128]{3,2,1,0:T(8,128)} %constant.11.clone.spread_h, ...), custom_call_target="tpu_custom_call" | custom-call | tf_op jit(solution)/shard_map/pallas_call | solution.py:279
  26.0 0.0 copy-start
  26.0 1.6 %copy.12 = f32[2,2,64,128]{3,2,1,0:T(8,128)} copy(f32[2,2,64,128]{3,2,1,0:T(8,128)} %get-tuple-element.4) | data formatting | bytes 262144
  27.5 0.0 copy-done
  27.6 0.6 %copy.13 = f32[1,1,16,64]{3,2,1,0:T(8,128)} copy(f32[1,1,16,64]{3,2,1,0:T(8,128)S(1)} %copy-done) | data formatting | bytes 8192
Async XLA Ops:
  26.0 1.6 %copy-start = (f32[1,1,16,64]{3,2,1,0:T(8,128)S(1)}, f32[1,1,16,64]{3,2,1,0:T(8,128)}, u32[]{:S(2)}) copy-start(f32[1,1,16,64]{3,2,1,0:T(8,128)} %get-tuple-element.5) | copy-start | bytes 12292

commit v3 on v2

--- a/solution.py
+++ b/solution.py
@@ -9,6 +9,7 @@
 from jax.sharding import PartitionSpec as P
 
 SWEEPS = 4
+BLOCKS = SWEEPS // 2
 OMEGA = 0.8
 COEF_X = 1.0
 COEF_Y = 1.0
@@ -59,8 +60,8 @@
 
 def kernel(
     wide, narrow, cot_h, obs_h, sig_h, lift_h, spread_h, green_h, mix_h, back_h, grad, coarse,
-    obs, sig, cc, ww, hx, hy, ys, lift, spread, green, mix, back, pack, recv,
-    tsem, sx, rx, sy, ry, sc, rc,
+    obs, sig, cc, ww, wl, hx, hc, hy, ys, hk, ks, ax, ay, lift, spread, green, mix, back, pack, recv,
+    tsem, sx, rx, sy, ry, sk, rk, sf, rf, sc, rc,
 ):
     dirs, cells_x, cells_y, cells_z = grad.shape
     last = cells_x - 1
@@ -104,102 +105,162 @@
 
         @pl.when(jnp.logical_not(edges[s]))
         def _():
-            for sweep in range(SWEEPS):
-                hx[sweep, s] = jnp.zeros(hx.shape[2:], jnp.float32)
+            hc[s] = jnp.zeros(hc.shape[1:], jnp.float32)
+            for block in range(BLOCKS):
+                hx[block, s] = jnp.zeros(hx.shape[2:], jnp.float32)
 
         @pl.when(jnp.logical_not(sides[s]))
         def _():
-            for sweep in range(SWEEPS):
-                hy[sweep, s] = jnp.zeros(hy.shape[2:], jnp.float32)
-
+            for block in range(BLOCKS):
+                hy[block, s] = jnp.zeros(hy.shape[2:], jnp.float32)
+
+        for t in range(2):
+
+            @pl.when(jnp.logical_not(edges[s] & sides[t]))
+            def _():
+                for block in range(BLOCKS):
+                    hk[block, s, t] = jnp.zeros(hk.shape[3:], jnp.float32)
+
+    ends = (0, last)
+    rims = (0, cells_y - 1)
     for load in loads[:3]:
         load.wait()
     for x in range(cells_x):
         share = OMEGA / (6.0 + sig[x])
         for d in range(dirs):
-            fluid = obs[d, x].astype(jnp.float32)
-            cc[x, d] = share * fluid
-
-    def wide_copy(sweep, s):
+            cc[x, d] = share * obs[d, x].astype(jnp.float32)
+
+    def beyond(s):
+        return w - 1 if s == 0 else w + 1
+
+    def across(t):
+        return n - 1 if t == 0 else n + 1
+
+    def remote(src, dst, sent, came, to):
         return pltpu.make_async_remote_copy(
-            src_ref=ww.at[sweep, 0 if s == 0 else last],
-            dst_ref=hx.at[sweep, 1 - s],
-            send_sem=sx.at[sweep, s],
-            recv_sem=rx.at[sweep, 1 - s],
-            device_id=(w - 1 if s == 0 else w + 1, n),
-            device_id_type=MESH,
-        )
-
-    def wide_arrival(sweep, s):
-        return pltpu.make_async_copy(hx.at[sweep, s], hx.at[sweep, s], rx.at[sweep, s])
-
-    def narrow_copy(sweep, s):
-        return pltpu.make_async_remote_copy(
-            src_ref=ys.at[sweep, s],
-            dst_ref=hy.at[sweep, 1 - s],
-            send_sem=sy.at[sweep, s],
-            recv_sem=ry.at[sweep, 1 - s],
-            device_id=(w, n - 1 if s == 0 else n + 1),
-            device_id_type=MESH,
-        )
-
-    def narrow_arrival(sweep, s):
-        return pltpu.make_async_copy(hy.at[sweep, s], hy.at[sweep, s], ry.at[sweep, s])
+            src_ref=src, dst_ref=dst, send_sem=sent, recv_sem=came, device_id=to, device_id_type=MESH
+        )
+
+    def copies(block):
+        made = []
+        for s in range(2):
+            made.append((
+                edges[s],
+                remote(ww.at[block], hx.at[block, 1 - s], sx.at[block, s], rx.at[block, 1 - s], (beyond(s), n)),
+                hx.at[block, s], rx.at[block, s],
+            ))
+        for t in range(2):
+            made.append((
+                sides[t],
+                remote(ys.at[block, t], hy.at[block, 1 - t], sy.at[block, t], ry.at[block, 1 - t], (w, across(t))),
+                hy.at[block, t], ry.at[block, t],
+            ))
+        for s in range(2):
+            for t in range(2):
+                made.append((
+                    edges[s] & sides[t],
+                    remote(
+                        ks.at[block, s, t], hk.at[block, 1 - s, 1 - t], sk.at[block, s, t],
+                        rk.at[block, 1 - s, 1 - t], (beyond(s), across(t)),
+                    ),
+                    hk.at[block, s, t], rk.at[block, s, t],
+                ))
+        if block == 0:
+            for s in range(2):
+                made.append((
+                    edges[s],
+                    remote(cc.at[ends[s]], hc.at[1 - s], sf.at[s], rf.at[1 - s], (beyond(s), n)),
+                    hc.at[s], rf.at[s],
+                ))
+        return made
 
     lane = lax.broadcasted_iota(jnp.int32, (cells_y, cells_z), 1)
     row = lax.broadcasted_iota(jnp.int32, (cells_y, cells_z), 0)
-    for sweep in range(SWEEPS):
+
+    def along_z(here):
+        index = lax.broadcasted_iota(jnp.int32, here.shape, 1)
+        return jnp.where(index == 0, 0.0, pltpu.roll(here, 1, 1)) + jnp.where(
+            index == cells_z - 1, 0.0, pltpu.roll(here, cells_z - 1, 1)
+        )
+
+    def along_y(here, low, high):
+        return jnp.where(row == 0, low, pltpu.roll(here, 1, 0)) + jnp.where(
+            row == cells_y - 1, high, pltpu.roll(here, cells_y - 1, 0)
+        )
+
+    def inner(src):
+        for x in range(cells_x):
+            for d in range(dirs):
+                here = src[x, d]
+                keep = jnp.where(cc[x, d] > 0.0, 1.0 - OMEGA, 1.0)
+                near = grad[d, x] * keep + along_z(here) + along_y(here, 0.0, 0.0)
+                if x > 0:
+                    near += src[x - 1, d]
+                if x < last:
+                    near += src[x + 1, d]
+                grad[d, x] = near
+
+    def outer(wide_side, narrow_side):
+        for x in range(cells_x):
+            for d in range(dirs):
+                r = x * dirs + d
+                for t in range(2):
+                    edge = pl.ds(rims[t], 1)
+                    grad[d, x, edge] += narrow_side[t, pl.ds(r, 1)]
+        for s in range(2):
+            for d in range(dirs):
+                grad[d, ends[s]] += wide_side[s, d]
+
+    planes = cells_x * dirs
+    for block in range(BLOCKS):
         for x in range(cells_x):
             for d in range(dirs):
                 value = cc[x, d] * grad[d, x]
-                ww[sweep, x, d] = value
-                ys[sweep, 0, x * dirs + d] = value[0]
-                ys[sweep, 1, x * dirs + d] = value[cells_y - 1]
-        if sweep == 0:
+                ww[block, x, d] = value
+                r = x * dirs + d
+                for t in range(2):
+                    step = 1 if t == 0 else -1
+                    ys[block, t, 0, r] = value[rims[t]]
+                    ys[block, t, 1, r] = value[rims[t] + step]
+                    ys[block, t, 2, r] = cc[x, d, rims[t]]
+                    for s in range(2):
+                        if x == ends[s]:
+                            ks[block, s, t, d] = value[rims[t]]
+        if block == 0:
             pl.semaphore_wait(barrier, total - 1)
-        for s in range(2):
-
-            @pl.when(edges[s])
-            def _():
-                wide_copy(sweep, s).start()
-
-            @pl.when(sides[s])
-            def _():
-                narrow_copy(sweep, s).start()
-
-        for x in range(cells_x):
-            for d in range(dirs):
-                here = ww[sweep, x, d]
-                keep = jnp.where(cc[x, d] > 0.0, 1.0 - OMEGA, 1.0)
-                near = grad[d, x] * keep
-                near += jnp.where(lane == 0, 0.0, pltpu.roll(here, 1, 1))
-                near += jnp.where(lane == cells_z - 1, 0.0, pltpu.roll(here, cells_z - 1, 1))
-                near += jnp.where(row == 0, 0.0, pltpu.roll(here, 1, 0))
-                near += jnp.where(row == cells_y - 1, 0.0, pltpu.roll(here, cells_y - 1, 0))
-                if x > 0:
-                    near += ww[sweep, x - 1, d]
-                if x < last:
-                    near += ww[sweep, x + 1, d]
-                grad[d, x] = near
-        for s in range(2):
-
-            @pl.when(sides[s])
-            def _():
-                narrow_arrival(sweep, s).wait()
-
+        made = copies(block)
+        for there, copy, _, _ in made:
+            pl.when(there)(copy.start)
+        inner(ww.at[block])
+        for there, _, buffer, came in made:
+            pl.when(there)(pltpu.make_async_copy(buffer, buffer, came).wait)
+
+        for s in range(2):
+            first = 1 - s
+            for d in range(dirs):
+                here = hx[block, s, ends[first], d]
+                around = hx[block, s, ends[first] - (1 if s == 0 else -1), d] + ww[block, ends[s], d]
+                around += along_z(here) + along_y(here, hk[block, s, 0, pl.ds(d, 1)], hk[block, s, 1, pl.ds(d, 1)])
+                ax[s, d] = (1.0 - OMEGA) * here + hc[s, d] * around
+        for t in range(2):
+            here = hy[block, t, 0]
+            left = jnp.concatenate([hk[block, 0, t], here[: planes - dirs]], axis=0)
+            right = jnp.concatenate([here[dirs:], hk[block, 1, t]], axis=0)
+            around = hy[block, t, 1] + ys[block, t, 0] + left + right + along_z(here)
+            ay[t] = (1.0 - OMEGA) * here + hy[block, t, 2] * around
         for x in range(cells_x):
             for d in range(dirs):
                 r = x * dirs + d
-                grad[d, x, 0:1] += hy[sweep, 0, r : r + 1]
-                grad[d, x, cells_y - 1 : cells_y] += hy[sweep, 1, r : r + 1]
-        for s in range(2):
-
-            @pl.when(edges[s])
-            def _():
-                wide_arrival(sweep, s).wait()
-
-            for d in range(dirs):
-                grad[d, 0 if s == 0 else last] += hx[sweep, s, d]
+                for t in range(2):
+                    grad[d, x, pl.ds(rims[t], 1)] += hy[block, t, 0, pl.ds(r, 1)]
+        for s in range(2):
+            for d in range(dirs):
+                grad[d, ends[s]] += hx[block, s, ends[1 - s], d]
+        for x in range(cells_x):
+            for d in range(dirs):
+                wl[x, d] = cc[x, d] * grad[d, x]
+        inner(wl)
+        outer(ax, ay)
 
     for load in loads[3:]:
         load.wait()
@@ -251,16 +312,9 @@
         both = jnp.where(column < h * width, both, wave[h * count_z : (h + 1) * count_z])
     coarse[0, 0] = dot(both, back[...])[:, 0 : coarse.shape[3]]
 
-    for sweep in range(SWEEPS):
-        for s in range(2):
-
-            @pl.when(edges[s])
-            def _():
-                wide_copy(sweep, s).wait_send()
-
-            @pl.when(sides[s])
-            def _():
-                narrow_copy(sweep, s).wait_send()
+    for block in range(BLOCKS):
+        for there, copy, _, _ in copies(block):
+            pl.when(there)(copy.wait_send)
 
     pltpu.make_async_copy(all_but_one, all_but_one, sc).wait()
 
@@ -288,10 +342,16 @@
             pltpu.VMEM(obstacle.shape, obstacle.dtype),
             pltpu.VMEM(sigma.shape, f32),
             pltpu.VMEM((cells_x, dirs) + plane, f32),
-            pltpu.VMEM((SWEEPS, cells_x, dirs) + plane, f32),
-            pltpu.VMEM((SWEEPS, 2, dirs) + plane, f32),
-            pltpu.VMEM((SWEEPS, 2, cells_x * dirs, cells_z), f32),
-            pltpu.VMEM((SWEEPS, 2, cells_x * dirs, cells_z), f32),
+            pltpu.VMEM((BLOCKS, cells_x, dirs) + plane, f32),
+            pltpu.VMEM((cells_x, dirs) + plane, f32),
+            pltpu.VMEM((BLOCKS, 2, cells_x, dirs) + plane, f32),
+            pltpu.VMEM((2, dirs) + plane, f32),
+            pltpu.VMEM((BLOCKS, 2, 3, cells_x * dirs, cells_z), f32),
+            pltpu.VMEM((BLOCKS, 2, 3, cells_x * dirs, cells_z), f32),
+            pltpu.VMEM((BLOCKS, 2, 2, dirs, cells_z), f32),
+            pltpu.VMEM((BLOCKS, 2, 2, dirs, cells_z), f32),
+            pltpu.VMEM((2, dirs) + plane, f32),
+            pltpu.VMEM((2, cells_x * dirs, cells_z), f32),
             pltpu.VMEM(lift.shape, f32),
             pltpu.VMEM(spread.shape[1:], f32),
             pltpu.VMEM(green.shape, f32),
@@ -300,10 +360,9 @@
             pltpu.VMEM((dirs, rows, LANES), f32),
             pltpu.VMEM((total, rows, LANES), f32),
             pltpu.SemaphoreType.DMA((8,)),
-            pltpu.SemaphoreType.DMA((SWEEPS, 2)),
-            pltpu.SemaphoreType.DMA((SWEEPS, 2)),
-            pltpu.SemaphoreType.DMA((SWEEPS, 2)),
-            pltpu.SemaphoreType.DMA((SWEEPS, 2)),
+            *[pltpu.SemaphoreType.DMA((BLOCKS, 2))] * 4,
+            *[pltpu.SemaphoreType.DMA((BLOCKS, 2, 2))] * 2,
+            *[pltpu.SemaphoreType.DMA((2,))] * 2,
             pltpu.SemaphoreType.DMA,
             pltpu.SemaphoreType.DMA,
         ],

time: 28.3 us -> 26 us (0.919)
  Pallas kernels: 25.3 us -> 23 us
    pallas_call x1, Pallas kernels: 25.3 us -> 23 us  [body(): pl.pallas_call(functools.partial(kernel, wide, narrow), out_shape=(jax.Sh...]
where the time goes in v3:
time: 26 us; the launch traced here: 25.8 us
  Pallas kernels  23 us (88%)
  local copies, waits for them, and re-layouts  2.18 us (8%)
  between operations  0.65 us (2%)
    pallas_call x1, Pallas kernels, body(): pl.pallas_call(functools.partial(kernel, wide, narrow), out_shape=(jax.Sh...  23 us
    unnamed x4, local copies, waits for them, and re-layouts  2.18 us

profile of v3, /device:TPU:0, one launch (start us, length us, event | category | flops | bytes accessed | tf_op | source)
XLA Modules:
  0.0 25.8 jit_solution(14131238329656319246)
XLA Ops:
  0.6 23.0 %shard_map.95 = (f32[2,2,64,128]{3,2,1,0:T(8,128)}, f32[1,1,16,64]{3,2,1,0:T(8,128)}) custom-call(f32[2,2,64,128]{3,2,1,0:T(8,128)} %cot_h.1, s32[2,2,64,128]{3,2,1,0:T(8,128)} %obs_h.1, f32[2,64,128]{2,1,0:T(8,128)} %sig_h.1, f32[16,128]{1,0:T(8,128)} %constant.10.clone.lift_h, f32[2,2,128,128]{3,2,1,0:T(8,128)} %constant.11.clone.spread_h, ...), custom_call_target="tpu_custom_call" | custom-call | tf_op jit(solution)/shard_map/pallas_call | solution.py:333
  23.7 0.0 copy-start
  23.7 1.6 %copy.12 = f32[2,2,64,128]{3,2,1,0:T(8,128)} copy(f32[2,2,64,128]{3,2,1,0:T(8,128)} %get-tuple-element.4) | data formatting | bytes 262144
  25.2 0.0 copy-done
  25.2 0.6 %copy.13 = f32[1,1,16,64]{3,2,1,0:T(8,128)} copy(f32[1,1,16,64]{3,2,1,0:T(8,128)S(1)} %copy-done) | data formatting | bytes 8192
Async XLA Ops:
  23.7 1.6 %copy-start = (f32[1,1,16,64]{3,2,1,0:T(8,128)S(1)}, f32[1,1,16,64]{3,2,1,0:T(8,128)}, u32[]{:S(2)}) copy-start(f32[1,1,16,64]{3,2,1,0:T(8,128)} %get-tuple-element.5) | copy-start | bytes 12292

commit v4 on v3

v4 whole, which is shorter than its diff:
```python
import functools

import jax
import jax.numpy as jnp
import numpy as np
from jax import lax
from jax.experimental import pallas as pl
from jax.experimental.pallas import tpu as pltpu
from jax.sharding import PartitionSpec as P

SWEEPS = 4
BLOCKS = SWEEPS // 2
OMEGA = 0.8
COEF_X = 1.0
COEF_Y = 1.0
COEF_Z = 4.0
SHIFT = 0.02
MESH = pl.DeviceIdType.MESH
LANES = 128


def sine(count):
    index = np.arange(count, dtype=np.int64) + 1
    product = index[:, None] * index[None, :] % (2 * (count + 1))
    return np.sqrt(2.0 / (count + 1)) * np.sin(np.pi * product / (count + 1))


def eigen(count):
    return 2.0 - 2.0 * np.cos(np.pi * (np.arange(count) + 1) / (count + 1))


def tables(cells_y, cells_z, narrow, coarse_x, coarse_y, coarse_z):
    part = LANES // coarse_y
    rows = coarse_z // part
    s_y, s_z = sine(coarse_y), sine(coarse_z)
    lift = np.repeat(s_z, cells_z // coarse_z, axis=0).T
    fine = np.repeat(s_y, 2, axis=0).reshape(narrow, cells_y, coarse_y)
    spread = np.tile(fine, (1, 1, part))
    plane = COEF_Y * eigen(coarse_y)[None, :] + COEF_Z * eigen(coarse_z)[:, None] + SHIFT
    plane = plane.reshape(part, rows, coarse_y).transpose(1, 0, 2).reshape(rows, LANES)
    steps = np.arange(2 * coarse_x + 1)
    wave = np.cos(np.pi * (np.outer(steps, np.arange(coarse_x) + 1) % (2 * coarse_x + 2)) / (coarse_x + 1))
    inverse = 1.0 / (COEF_X * eigen(coarse_x)[:, None] + plane.reshape(1, -1))
    green = (wave @ inverse / (coarse_x + 1)).reshape(-1, rows, LANES)
    mix = np.zeros((part * coarse_z, LANES))
    mix[:, :rows] = s_z.reshape(coarse_z, part, rows).transpose(1, 0, 2).reshape(part * coarse_z, rows)
    back = np.zeros((LANES, LANES))
    back[:, :coarse_y] = np.tile(s_y, (part, 1))
    return [np.asarray(t, np.float32) for t in (lift, spread, green, mix, back)]


def dot(a, b, dims=((1,), (0,))):
    return lax.dot_general(
        a, b, (dims, ((), ())), precision=lax.Precision.HIGHEST, preferred_element_type=jnp.float32
    )


def kernel(
    wide, narrow, cot_h, obs_h, sig_h, lift_h, spread_h, green_h, mix_h, back_h, grad_h, coarse,
    grad, obs, sig, cc, ww, wl, hx, hc, hy, ys, hk, ks, ax, ay, lift, spread, green, mix, back, pack, recv,
    tsem, sx, rx, sy, ry, sk, rk, sf, rf, osem, sc, rc,
):
    dirs, cells_x, cells_y, cells_z = grad.shape
    last = cells_x - 1
    w = lax.axis_index("wide")
    n = lax.axis_index("narrow")
    total = wide * narrow
    me = w * narrow + n

    loads = [
        pltpu.make_async_copy(src, dst, tsem.at[i])
        for i, (src, dst) in enumerate(
            (
                (sig_h, sig),
                (obs_h, obs),
                (cot_h, grad),
                (lift_h, lift),
                (spread_h.at[n], spread),
                (green_h, green),
                (mix_h, mix),
                (back_h, back),
            )
        )
    ]
    for load in loads:
        load.start()

    barrier = pltpu.get_barrier_semaphore()

    def greet(k, carry):
        peer = lax.rem(me + k, total)
        pl.semaphore_signal(
            barrier, inc=1, device_id=(lax.div(peer, narrow), lax.rem(peer, narrow)), device_id_type=MESH
        )
        return carry

    lax.fori_loop(1, total, greet, 0)

    edges = (w > 0, w < wide - 1)
    sides = (n > 0, n < narrow - 1)
    for s in range(2):

        @pl.when(jnp.logical_not(edges[s]))
        def _():
            hc[s] = jnp.zeros(hc.shape[1:], jnp.float32)
            for block in range(BLOCKS):
                hx[block, s] = jnp.zeros(hx.shape[2:], jnp.float32)

        @pl.when(jnp.logical_not(sides[s]))
        def _():
            for block in range(BLOCKS):
                hy[block, s] = jnp.zeros(hy.shape[2:], jnp.float32)

        for t in range(2):

            @pl.when(jnp.logical_not(edges[s] & sides[t]))
            def _():
                for block in range(BLOCKS):
                    hk[block, s, t] = jnp.zeros(hk.shape[3:], jnp.float32)

    ends = (0, last)
    rims = (0, cells_y - 1)
    for load in loads[:3]:
        load.wait()
    for x in range(cells_x):
        share = OMEGA / (6.0 + sig[x])
        for d in range(dirs):
            cc[x, d] = share * obs[d, x].astype(jnp.float32)

    def beyond(s):
        return w - 1 if s == 0 else w + 1

    def across(t):
        return n - 1 if t == 0 else n + 1

    def remote(src, dst, sent, came, to):
        return pltpu.make_async_remote_copy(
            src_ref=src, dst_ref=dst, send_sem=sent, recv_sem=came, device_id=to, device_id_type=MESH
        )

    def copies(block, d):
        made = []
        for s in range(2):
            made.append((
                edges[s],
                remote(
                    ww.at[block, :, d], hx.at[block, 1 - s, :, d], sx.at[block, s, d], rx.at[block, 1 - s, d],
                    (beyond(s), n),
                ),
                hx.at[block, s, :, d], rx.at[block, s, d],
            ))
        for t in range(2):
            made.append((
                sides[t],
                remote(
                    ys.at[block, t, d], hy.at[block, 1 - t, d], sy.at[block, t, d], ry.at[block, 1 - t, d],
                    (w, across(t)),
                ),
                hy.at[block, t, d], ry.at[block, t, d],
            ))
        for s in range(2):
            for t in range(2):
                made.append((
                    edges[s] & sides[t],
                    remote(
                        ks.at[block, s, t, d], hk.at[block, 1 - s, 1 - t, d], sk.at[block, s, t, d],
                        rk.at[block, 1 - s, 1 - t, d], (beyond(s), across(t)),
                    ),
                    hk.at[block, s, t, d], rk.at[block, s, t, d],
                ))
        if block == 0:
            for s in range(2):
                made.append((
                    edges[s],
                    remote(cc.at[ends[s], d], hc.at[1 - s, d], sf.at[s, d], rf.at[1 - s, d], (beyond(s), n)),
                    hc.at[s, d], rf.at[s, d],
                ))
        return made

    lane = lax.broadcasted_iota(jnp.int32, (cells_y, cells_z), 1)
    row = lax.broadcasted_iota(jnp.int32, (cells_y, cells_z), 0)

    def along_z(here):
        index = lax.broadcasted_iota(jnp.int32, here.shape, 1)
        return jnp.where(index == 0, 0.0, pltpu.roll(here, 1, 1)) + jnp.where(
            index == cells_z - 1, 0.0, pltpu.roll(here, cells_z - 1, 1)
        )

    def along_y(here, low, high):
        return jnp.where(row == 0, low, pltpu.roll(here, 1, 0)) + jnp.where(
            row == cells_y - 1, high, pltpu.roll(here, cells_y - 1, 0)
        )

    def inner(src, d):
        for x in range(cells_x):
            here = src[x, d]
            keep = jnp.where(cc[x, d] > 0.0, 1.0 - OMEGA, 1.0)
            near = grad[d, x] * keep + along_z(here) + along_y(here, 0.0, 0.0)
            if x > 0:
                near += src[x - 1, d]
            if x < last:
                near += src[x + 1, d]
            grad[d, x] = near

    def begin(block, d):
        for x in range(cells_x):
            value = cc[x, d] * grad[d, x]
            ww[block, x, d] = value
            for t in range(2):
                step = 1 if t == 0 else -1
                ys[block, t, d, 0, x] = value[rims[t]]
                ys[block, t, d, 1, x] = value[rims[t] + step]
                ys[block, t, d, 2, x] = cc[x, d, rims[t]]
                for s in range(2):
                    if x == ends[s]:
                        ks[block, s, t, d, 0] = value[rims[t]]

    def launch(block, d):
        for there, copy, _, _ in copies(block, d):
            pl.when(there)(copy.start)

    def finish(block, d):
        for there, _, buffer, came in copies(block, d):
            pl.when(there)(pltpu.make_async_copy(buffer, buffer, came).wait)
        for s in range(2):
            near_at = ends[1 - s]
            far_at = near_at - (1 if s == 0 else -1)
            here = hx[block, s, near_at, d]
            around = hx[block, s, far_at, d] + ww[block, ends[s], d]
            around += along_z(here) + along_y(here, hk[block, s, 0, d], hk[block, s, 1, d])
            ax[s, d] = (1.0 - OMEGA) * here + hc[s, d] * around
            grad[d, ends[s]] += here
        for t in range(2):
            here = hy[block, t, d, 0]
            left = jnp.concatenate([hk[block, 0, t, d], here[: cells_x - 1]], axis=0)
            right = jnp.concatenate([here[1:], hk[block, 1, t, d]], axis=0)
            around = hy[block, t, d, 1] + ys[block, t, d, 0] + left + right + along_z(here)
            ay[t, d] = (1.0 - OMEGA) * here + hy[block, t, d, 2] * around
            for x in range(cells_x):
                grad[d, x, pl.ds(rims[t], 1)] += hy[block, t, d, 0, pl.ds(x, 1)]
        for x in range(cells_x):
            wl[x, d] = cc[x, d] * grad[d, x]
        inner(wl, d)
        for t in range(2):
            for x in range(cells_x):
                grad[d, x, pl.ds(rims[t], 1)] += ay[t, d, pl.ds(x, 1)]
        for s in range(2):
            grad[d, ends[s]] += ax[s, d]

    rows = recv.shape[1]
    part = lift.shape[0] // rows
    width = LANES // part
    column = lax.broadcasted_iota(jnp.int32, (rows, LANES), 1)

    def give(d):
        slab = sum(grad[d, x] for x in range(cells_x))
        wave = dot(dot(lift[...], slab, ((1,), (1,))), spread[...])
        packed = wave[0:rows]
        for h in range(1, part):
            packed = jnp.where(column < h * width, packed, wave[h * rows : (h + 1) * rows])
        pack[d] = packed
        owner = d // (dirs // narrow)

        def send(k, carry):
            pltpu.make_async_remote_copy(
                src_ref=pack.at[d],
                dst_ref=recv.at[me],
                send_sem=sc,
                recv_sem=rc,
                device_id=(lax.rem(w + k, wide), owner),
                device_id_type=MESH,
            ).start()
            return carry

        lax.fori_loop(1, wide, send, 0)

        @pl.when(n != owner)
        def _():
            send(0, 0)

        @pl.when(n == owner)
        def _():
            recv[me] = packed

    for d in range(dirs):
        begin(0, d)
        if d == 0:
            pl.semaphore_wait(barrier, total - 1)
        launch(0, d)
    for d in range(dirs):
        inner(ww.at[0], d)
    for load in loads[3:]:
        load.wait()
    stores = []
    for block in range(BLOCKS):
        for d in range(dirs):
            finish(block, d)
            if block + 1 < BLOCKS:
                begin(block + 1, d)
                launch(block + 1, d)
                inner(ww.at[block + 1], d)
            else:
                give(d)
                stores.append(pltpu.make_async_copy(grad.at[d], grad_h.at[d], osem.at[d]))
                stores[-1].start()

    all_but_one = recv.at[pl.ds(0, total - 1)]
    pltpu.make_async_copy(all_but_one, all_but_one, rc).wait()

    def solve(x, carry):
        near = green[lax.abs(w - x)] - green[w + x + 2]
        field = recv[x * narrow]
        for m in range(1, narrow):
            field += recv[x * narrow + m]
        return carry + near * field

    solved = lax.fori_loop(0, wide, solve, jnp.zeros((rows, LANES), jnp.float32), unroll=min(wide, 16))
    wave = dot(mix[:, 0:rows], solved)
    count_z = coarse.shape[2]
    column = lax.broadcasted_iota(jnp.int32, (count_z, LANES), 1)
    both = wave[0:count_z]
    for h in range(1, part):
        both = jnp.where(column < h * width, both, wave[h * count_z : (h + 1) * count_z])
    coarse[0, 0] = dot(both, back[...])[:, 0 : coarse.shape[3]]

    for block in range(BLOCKS):
        for d in range(dirs):
            for there, copy, _, _ in copies(block, d):
                pl.when(there)(copy.wait_send)
    for store in stores:
        store.wait()

    pltpu.make_async_copy(all_but_one, all_but_one, sc).wait()


def body(wide, narrow, fine_cot, obstacle, sigma):
    dirs, cells_x, cells_y, cells_z = fine_cot.shape
    coarse_x, coarse_y, coarse_z = wide * cells_x // 2, narrow * cells_y // 2, cells_z // 8
    made = tables(cells_y, cells_z, narrow, coarse_x, coarse_y, coarse_z)
    lift, spread, green, mix, back = made
    total = wide * narrow
    rows = green.shape[1]
    f32 = jnp.float32
    vmem = pl.BlockSpec(memory_space=pltpu.VMEM)
    stay = pl.BlockSpec(memory_space=pl.ANY)
    plane = (cells_y, cells_z)
    return pl.pallas_call(
        functools.partial(kernel, wide, narrow),
        out_shape=(
            jax.ShapeDtypeStruct(fine_cot.shape, f32),
            jax.ShapeDtypeStruct((1, 1, coarse_z, coarse_y), f32),
        ),
        in_specs=[stay] * 8,
        out_specs=(stay, vmem),
        scratch_shapes=[
            pltpu.VMEM(fine_cot.shape, f32),
            pltpu.VMEM(obstacle.shape, obstacle.dtype),
            pltpu.VMEM(sigma.shape, f32),
            pltpu.VMEM((cells_x, dirs) + plane, f32),
            pltpu.VMEM((BLOCKS, cells_x, dirs) + plane, f32),
            pltpu.VMEM((cells_x, dirs) + plane, f32),
            pltpu.VMEM((BLOCKS, 2, cells_x, dirs) + plane, f32),
            pltpu.VMEM((2, dirs) + plane, f32),
            pltpu.VMEM((BLOCKS, 2, dirs, 3, cells_x, cells_z), f32),
            pltpu.VMEM((BLOCKS, 2, dirs, 3, cells_x, cells_z), f32),
            pltpu.VMEM((BLOCKS, 2, 2, dirs, 1, cells_z), f32),
            pltpu.VMEM((BLOCKS, 2, 2, dirs, 1, cells_z), f32),
            pltpu.VMEM((2, dirs) + plane, f32),
            pltpu.VMEM((2, dirs, cells_x, cells_z), f32),
            pltpu.VMEM(lift.shape, f32),
            pltpu.VMEM(spread.shape[1:], f32),
            pltpu.VMEM(green.shape, f32),
            pltpu.VMEM(mix.shape, f32),
            pltpu.VMEM(back.shape, f32),
            pltpu.VMEM((dirs, rows, LANES), f32),
            pltpu.VMEM((total, rows, LANES), f32),
            pltpu.SemaphoreType.DMA((8,)),
            *[pltpu.SemaphoreType.DMA((BLOCKS, 2, dirs))] * 4,
            *[pltpu.SemaphoreType.DMA((BLOCKS, 2, 2, dirs))] * 2,
            *[pltpu.SemaphoreType.DMA((2, dirs))] * 2,
            pltpu.SemaphoreType.DMA((dirs,)),
            pltpu.SemaphoreType.DMA,
            pltpu.SemaphoreType.DMA,
        ],
        compiler_params=pltpu.CompilerParams(
            collective_id=0, has_side_effects=True, vmem_limit_bytes=60 * 2**20
        ),
    )(fine_cot, obstacle, sigma, *made)


def solution(mesh):
    placed = (
        P(None, "wide", "narrow", None),
        P(None, "wide", "narrow", None),
        P("wide", "narrow", None),
    )
    return jax.shard_map(
        functools.partial(body, mesh.shape["wide"], mesh.shape["narrow"]),
        mesh=mesh,
        in_specs=placed,
        out_specs=(P(None, "wide", "narrow", None), P("wide", "narrow", None, None)),
        check_vma=False,
    )
```

time: 26 us -> 24.3 us (0.935)
  Pallas kernels: 23 us -> 21.3 us
    pallas_call x1, Pallas kernels: 23 us -> 21.3 us  [body(): pl.pallas_call(functools.partial(kernel, wide, narrow), out_shape=(jax.Sh...]
where the time goes in v4:
time: 24.3 us; the launch traced here: 24.1 us
  Pallas kernels  21.3 us (88%)
  local copies, waits for them, and re-layouts  2.18 us (9%)
  between operations  0.65 us (3%)
    pallas_call x1, Pallas kernels, body(): pl.pallas_call(functools.partial(kernel, wide, narrow), out_shape=(jax.Sh...  21.3 us
    unnamed x4, local copies, waits for them, and re-layouts  2.18 us

profile of v4, /device:TPU:0, one launch (start us, length us, event | category | flops | bytes accessed | tf_op | source)
XLA Modules:
  0.0 24.1 jit_solution(18244465488657738229)
XLA Ops:
  0.6 21.3 %shard_map.95 = (f32[2,2,64,128]{3,2,1,0:T(8,128)}, f32[1,1,16,64]{3,2,1,0:T(8,128)}) custom-call(f32[2,2,64,128]{3,2,1,0:T(8,128)} %cot_h.1, s32[2,2,64,128]{3,2,1,0:T(8,128)} %obs_h.1, f32[2,64,128]{2,1,0:T(8,128)} %sig_h.1, f32[16,128]{1,0:T(8,128)} %constant.10.clone.lift_h, f32[2,64,128]{2,1,0:T(8,128)} %constant.11.clone.spread_h, ...), custom_call_target="tpu_custom_call" | custom-call | tf_op jit(solution)/shard_map/pallas_call | solution.py:347
  21.9 0.0 copy-start
  21.9 1.6 %copy.12 = f32[2,2,64,128]{3,2,1,0:T(8,128)} copy(f32[2,2,64,128]{3,2,1,0:T(8,128)} %get-tuple-element.4) | data formatting | bytes 262144
  23.5 0.0 copy-done
  23.5 0.6 %copy.13 = f32[1,1,16,64]{3,2,1,0:T(8,128)} copy(f32[1,1,16,64]{3,2,1,0:T(8,128)S(1)} %copy-done) | data formatting | bytes 8192
Async XLA Ops:
  21.9 1.6 %copy-start = (f32[1,1,16,64]{3,2,1,0:T(8,128)S(1)}, f32[1,1,16,64]{3,2,1,0:T(8,128)}, u32[]{:S(2)}) copy-start(f32[1,1,16,64]{3,2,1,0:T(8,128)} %get-tuple-element.5) | copy-start | bytes 12292

commit v5 on v4

--- a/solution.py
+++ b/solution.py
@@ -56,7 +56,7 @@
 
 
 def kernel(
-    wide, narrow, cot_h, obs_h, sig_h, lift_h, spread_h, green_h, mix_h, back_h, grad_h, coarse,
+    wide, narrow, cot_h, obs_h, sig_h, table_h, grad_h, coarse,
     grad, obs, sig, cc, ww, wl, hx, hc, hy, ys, hk, ks, ax, ay, lift, spread, green, mix, back, pack, recv,
     tsem, sx, rx, sy, ry, sk, rk, sf, rf, osem, sc, rc,
 ):
@@ -67,6 +67,12 @@
     total = wide * narrow
     me = w * narrow + n
 
+    starts = np.cumsum([0, lift.shape[0], narrow * cells_y, green.shape[0], mix.shape[0]]).tolist()
+
+    def rows_of(i, dst):
+        first = starts[i] + (pl.multiple_of(n * cells_y, 8) if i == 1 else 0)
+        return table_h.at[pl.ds(first, dst.shape[0])], dst
+
     loads = [
         pltpu.make_async_copy(src, dst, tsem.at[i])
         for i, (src, dst) in enumerate(
@@ -74,11 +80,11 @@
                 (sig_h, sig),
                 (obs_h, obs),
                 (cot_h, grad),
-                (lift_h, lift),
-                (spread_h.at[n], spread),
-                (green_h, green),
-                (mix_h, mix),
-                (back_h, back),
+                rows_of(0, lift),
+                rows_of(1, spread),
+                rows_of(2, green),
+                rows_of(3, mix),
+                rows_of(4, back),
             )
         )
     ]
@@ -216,7 +222,8 @@
                         ks[block, s, t, d, 0] = value[rims[t]]
 
     def launch(block, d):
-        for there, copy, _, _ in copies(block, d):
+        made = copies(block, d)
+        for there, copy, _, _ in made[2:8] + made[:2] + made[8:]:
             pl.when(there)(copy.start)
 
     def finish(block, d):
@@ -308,7 +315,8 @@
     pltpu.make_async_copy(all_but_one, all_but_one, rc).wait()
 
     def solve(x, carry):
-        near = green[lax.abs(w - x)] - green[w + x + 2]
+        near = green[pl.ds(pl.multiple_of(lax.abs(w - x) * rows, 8), rows)]
+        near -= green[pl.ds(pl.multiple_of((w + x + 2) * rows, 8), rows)]
         field = recv[x * narrow]
         for m in range(1, narrow):
             field += recv[x * narrow + m]
@@ -340,6 +348,8 @@
     lift, spread, green, mix, back = made
     total = wide * narrow
     rows = green.shape[1]
+    green = green.reshape(-1, LANES)
+    table = np.concatenate([lift, spread.reshape(-1, LANES), green, mix, back], axis=0)
     f32 = jnp.float32
     vmem = pl.BlockSpec(memory_space=pltpu.VMEM)
     stay = pl.BlockSpec(memory_space=pl.ANY)
@@ -350,7 +360,7 @@
             jax.ShapeDtypeStruct(fine_cot.shape, f32),
             jax.ShapeDtypeStruct((1, 1, coarse_z, coarse_y), f32),
         ),
-        in_specs=[stay] * 8,
+        in_specs=[stay] * 4,
         out_specs=(stay, vmem),
         scratch_shapes=[
             pltpu.VMEM(fine_cot.shape, f32),
@@ -383,9 +393,9 @@
             pltpu.SemaphoreType.DMA,
         ],
         compiler_params=pltpu.CompilerParams(
-            collective_id=0, has_side_effects=True, vmem_limit_bytes=60 * 2**20
+            collective_id=0, has_side_effects=True, vmem_limit_bytes=55050 * 2**10
         ),
-    )(fine_cot, obstacle, sigma, *made)
+    )(fine_cot, obstacle, sigma, table)
 
 
 def solution(mesh):

time: 24.3 us -> 24.2 us (level)
  Pallas kernels: 21.3 us -> 20.3 us
  local copies, waits for them, and re-layouts: 2.18 us -> 3 us
    pallas_call x1, Pallas kernels: 21.3 us -> 20.3 us  [body(): pl.pallas_call(functools.partial(kernel, wide, narrow), out_shape=(jax.Sh...]
    unnamed x4, local copies, waits for them, and re-layouts: 2.18 us -> 3 us
where the time goes in v5:
time: 24.2 us; the launch traced here: 24 us
  Pallas kernels  20.3 us (84%)
  local copies, waits for them, and re-layouts  3 us (12%)
  between operations  0.65 us (3%)
    pallas_call x1, Pallas kernels, body(): pl.pallas_call(functools.partial(kernel, wide, narrow), out_shape=(jax.Sh...  20.3 us
    unnamed x4, local copies, waits for them, and re-layouts  3 us

profile of v5, /device:TPU:0, one launch (start us, length us, event | category | flops | bytes accessed | tf_op | source)
XLA Modules:
  0.0 24.0 jit_solution(3690018135516310047)
XLA Ops:
  0.6 0.0 copy-start
  0.6 0.8 %copy-done = f32[2,64,128]{2,1,0:T(8,128)S(1)} copy-done((f32[2,64,128]{2,1,0:T(8,128)S(1)}, f32[2,64,128]{2,1,0:T(8,128)}, u32[]{:S(2)}) %copy-start) | copy-done | bytes 65560
  1.5 20.3 %shard_map.59 = (f32[2,2,64,128]{3,2,1,0:T(8,128)}, f32[1,1,16,64]{3,2,1,0:T(8,128)S(1)}) custom-call(f32[2,2,64,128]{3,2,1,0:T(8,128)} %cot_h.1, s32[2,2,64,128]{3,2,1,0:T(8,128)} %obs_h.1, f32[2,64,128]{2,1,0:T(8,128)S(1)} %copy-done, f32[568,128]{1,0:T(8,128)} %constant.2.clone.table_h), custom_call_target="tpu_custom_call" | custom-call | tf_op jit(solution)/shard_map/pallas_call | solution.py:357
  21.8 1.6 %copy.8 = f32[2,2,64,128]{3,2,1,0:T(8,128)} copy(f32[2,2,64,128]{3,2,1,0:T(8,128)} %get-tuple-element.4) | data formatting | bytes 262144
  23.4 0.6 %copy.9 = f32[1,1,16,64]{3,2,1,0:T(8,128)} copy(f32[1,1,16,64]{3,2,1,0:T(8,128)S(1)} %get-tuple-element.5) | data formatting | bytes 8192
Async XLA Ops:
  0.6 0.8 %copy-start = (f32[2,64,128]{2,1,0:T(8,128)S(1)}, f32[2,64,128]{2,1,0:T(8,128)}, u32[]{:S(2)}) copy-start(f32[2,64,128]{2,1,0:T(8,128)} %sig_h.1) | copy-start | bytes 196612
